TPU v7x, 128 devices: a whole 4x4x4 slice. The times are simulated.
128 devices in a mesh: gx: 8 (over x_lo, z), gy: 16 (over x_hi, y, core).
Axes of the slice: x: 4 (x_hi: 2, x_lo: 2; x = x_hi * 2 + x_lo), y: 4, z: 4, core: 2. Of those that a mesh axis runs over, the one named last changes fastest.
Arguments:
- ocean_forcing: float32 [16384, 4, 8, 128], P(('gx', 'gy')), may hold values from -3 to 3
- route: int32 [16384], replicated, may hold values from 0 to 16383, as said below
- land_mask: int32 [2048, 8192], P('gy', 'gx'), may hold values 0 or 1
- mass: float32 [2048, 8192], P('gy', 'gx'), may hold values from 2 to 4
- strength: float32 [2048, 8192], P('gy', 'gx'), may hold values from 1 to 2
- velocity_start: float32 [2, 2048, 8192], P(None, 'gy', 'gx'), may hold values from -4 to 4
- stress_start: float32 [3, 2048, 8192], P(None, 'gy', 'gx'), may hold values from -4 to 4
Outputs:
- ocean_velocity: float32 [16384, 2, 8, 128], P(('gx', 'gy'))
- ice_stress: float32 [3, 2048, 8192], P(None, 'gy', 'gx')
Inputs may be any that keep to these rules, and one draw needn't show every extreme that they name: route is a permutation of the 16384 tile numbers; the 128 tiles of each ocean device (aligned blocks of 128 entries) go exactly 2 each to 64 ice blocks (ice block route[t] // 128) and to no others.
All inputs are finite; a program needn't handle non-finite values. No bound on the sum of `land_mask` on one device may be relied on, other than what follows from the above.
Results may differ from a plain program's by a relative error of at most 0.00002.
Values sent between devices are 32-bit elements; how exact they have to be, the bound alone decides.
A program may use at most 64 MiB of HBM per device.

v0:
```python
import jax
import jax.numpy as jnp
from jax import lax
from jax.sharding import PartitionSpec as P

ITERS = 16


relax_rate = 0.1
floor_square = 1.0
drag_rate = 0.5
turn_rate = 0.3
tilt_weight = 0.05


def padded(shard, sides, width, wrap):
    for axis, dim in sides:
        count, length = (lax.axis_size(axis), shard.shape[dim])
        up = [(i, (i + 1) % count) for i in range(count if wrap else count - 1)]
        down = [(j, i) for i, j in up]
        last = lax.slice_in_dim(shard, length - width, length, axis=dim)
        leading = lax.slice_in_dim(shard, 0, width, axis=dim)
        before = lax.ppermute(last, axis, up)
        after = lax.ppermute(leading, axis, down)
        shard = jnp.concatenate([before, shard, after], axis=dim)
    return shard


def from_partner(shard, axis, apart):
    return lax.ppermute(shard, axis, [(i, i ^ 1 << apart) for i in range(lax.axis_size(axis))])


def advance(extended, strength_ext, mass, force_x, force_y, share):
    zonal = extended[0]
    merid = extended[1]
    stress_sum = extended[2]
    stress_diff = extended[3]
    stress_shear = extended[4]
    zonal_dx = 0.5 * (zonal[1:-1, 2:] - zonal[1:-1, :-2])
    zonal_dy = 0.5 * (zonal[2:, 1:-1] - zonal[:-2, 1:-1])
    merid_dx = 0.5 * (merid[1:-1, 2:] - merid[1:-1, :-2])
    merid_dy = 0.5 * (merid[2:, 1:-1] - merid[:-2, 1:-1])
    divergence = zonal_dx + merid_dy
    tension = zonal_dx - merid_dy
    shearing = zonal_dy + merid_dx
    strain_size = jnp.sqrt(
        divergence * divergence + 0.25 * (tension * tension + shearing * shearing) + floor_square
    )
    viscous = relax_rate * strength_ext[1:-1, 1:-1] / strain_size
    new_sum = (stress_sum[1:-1, 1:-1] + viscous * (divergence - strain_size)) / (1.0 + relax_rate)
    new_diff = (stress_diff[1:-1, 1:-1] + 0.25 * viscous * tension) / (1.0 + relax_rate)
    new_shear = (stress_shear[1:-1, 1:-1] + 0.125 * viscous * shearing) / (1.0 + relax_rate)
    normal_xx = 0.5 * (new_sum + new_diff)
    normal_yy = 0.5 * (new_sum - new_diff)
    push_x = 0.5 * (normal_xx[1:-1, 2:] - normal_xx[1:-1, :-2]) + 0.5 * (
        new_shear[2:, 1:-1] - new_shear[:-2, 1:-1]
    )
    push_y = 0.5 * (new_shear[1:-1, 2:] - new_shear[1:-1, :-2]) + 0.5 * (
        normal_yy[2:, 1:-1] - normal_yy[:-2, 1:-1]
    )
    right_x = mass * zonal[2:-2, 2:-2] + push_x + force_x
    right_y = mass * merid[2:-2, 2:-2] + push_y + force_y
    damping = mass + drag_rate
    turning = turn_rate * mass
    determinant = damping * damping + turning * turning
    zonal_new = (damping * right_x + turning * right_y) / determinant * share
    merid_new = (damping * right_y - turning * right_x) / determinant * share
    return jnp.stack(
        [zonal_new, merid_new, new_sum[1:-1, 1:-1], new_diff[1:-1, 1:-1], new_shear[1:-1, 1:-1]]
    )


def extend(field, signs, margin):
    cycle = padded(field, (("gx", 2),), margin, True)
    framed = padded(cycle, (("gy", 1),), margin, False)
    mirror = cycle[:, -margin:, :]
    for level in range(lax.axis_size("gx").bit_length() - 1):
        mirror = from_partner(mirror, "gx", level)
    folded = jnp.flip(mirror, axis=(1, 2)) * signs[:, None, None]
    summit = lax.axis_index("gy") == lax.axis_size("gy") - 1
    north = jnp.where(summit, folded, framed[:, -margin:, :])
    return jnp.concatenate([framed[:, :-margin, :], north], axis=1)


def pack_slots(tiles, slot_of, count):
    hits = slot_of[None, :] == jnp.arange(count, dtype=jnp.int32)[:, None]
    source = jnp.sum(
        jnp.where(hits, jnp.arange(tiles.shape[0], dtype=jnp.int32)[None, :], 0), axis=1
    )
    filled = jnp.any(hits, axis=1)
    picked = jnp.take(tiles, source, axis=0)
    return jnp.where(filled[:, None, None, None], picked, 0.0)


def local(ocean_forcing, route, land_mask, mass, strength, velocity_start, stress_start):
    column_blocks = lax.axis_size("gx")
    row_blocks = lax.axis_size("gy")
    blocks = column_blocks * row_blocks
    per_block = ocean_forcing.shape[0]
    depth = 2 * per_block // blocks
    slots = blocks * depth
    tile_rows = ocean_forcing.shape[2]
    tile_cols = ocean_forcing.shape[3]
    height = land_mask.shape[0]
    width = land_mask.shape[1]
    across = width // tile_cols
    down = per_block // across
    device = lax.axis_index("gx") * row_blocks + lax.axis_index("gy")
    table = route.reshape(blocks, per_block)
    owners = table // per_block
    my_owners = lax.dynamic_index_in_dim(owners, device, 0, keepdims=False)
    chosen = (my_owners[:, None] == jnp.arange(blocks, dtype=jnp.int32)[None, :]).astype(jnp.int32)
    send_rank = jnp.sum((jnp.cumsum(chosen, axis=0) - 1) * chosen, axis=1)
    send_slot = my_owners * depth + send_rank
    outgoing = pack_slots(ocean_forcing, send_slot, slots)
    arrived = lax.all_to_all(outgoing, ("gx", "gy"), split_axis=0, concat_axis=0, tiled=True)
    anchor = (
        jnp.zeros((blocks * per_block,), jnp.int32)
        .at[route]
        .set(jnp.arange(blocks * per_block, dtype=jnp.int32))
    )
    mine_anchor = lax.dynamic_slice_in_dim(anchor, device * per_block, per_block)
    arriving = (owners == device).astype(jnp.int32)
    arrive_rank = (jnp.cumsum(arriving, axis=1) - 1).reshape(-1)
    recv_slot = mine_anchor // per_block * depth + jnp.take(arrive_rank, mine_anchor)
    ice_tiles = jnp.take(arrived, recv_slot, axis=0)
    ice_forcing = (
        ice_tiles.reshape(down, across, 4, tile_rows, tile_cols)
        .transpose(2, 0, 3, 1, 4)
        .reshape(4, height, width)
    )
    force_x = ice_forcing[0] + tilt_weight * mass * ice_forcing[2]
    force_y = ice_forcing[1] + tilt_weight * mass * ice_forcing[3]
    share = land_mask.astype(jnp.float32)
    signs = jnp.array([-1.0, -1.0, 1.0, 1.0, 1.0], jnp.float32)
    state = jnp.concatenate([velocity_start * share[None], stress_start], axis=0)
    strength_ext = extend(strength[None], jnp.ones((1,), jnp.float32), 2)[0]

    def sweep(count, current):
        return advance(extend(current, signs, 2), strength_ext, mass, force_x, force_y, share)

    state = lax.fori_loop(0, ITERS, sweep, state)
    velocity = state[:2]
    ice_out = (
        velocity.reshape(2, down, tile_rows, across, tile_cols)
        .transpose(1, 3, 0, 2, 4)
        .reshape(per_block, 2, tile_rows, tile_cols)
    )
    returning = pack_slots(ice_out, recv_slot, slots)
    came_back = lax.all_to_all(returning, ("gx", "gy"), split_axis=0, concat_axis=0, tiled=True)
    ocean_velocity = jnp.take(came_back, send_slot, axis=0)
    return (ocean_velocity, state[2:])


def solution(mesh):
    placed = (
        P(("gx", "gy"), None, None, None),
        P(),
        P("gy", "gx"),
        P("gy", "gx"),
        P("gy", "gx"),
        P(None, "gy", "gx"),
        P(None, "gy", "gx"),
    )
    return jax.shard_map(
        local,
        mesh=mesh,
        in_specs=placed,
        out_specs=(P(("gx", "gy"), None, None, None), P(None, "gy", "gx")),
        check_vma=False,
    )
```

profile of v0, /device:TPU:1, one launch (start us, length us, event | category | flops | bytes accessed | tf_op | source)
XLA Modules:
  0.0 940.1 jit_solution(7505176205936572192)
XLA Ops:
  10.0 12.0 %all-to-all-start = ((f32[256,4,8,128]{3,2,1,0:T(8,128)}), f32[256,4,8,128]{3,2,1,0:T(8,128)}, u32[]{:S(2)}, u32[]{:S(2)}) async-start(f32[256,4,8,128]{3,2,1,0:T(8,128)} %select_select_fusion), calls=%async_computation | async-start | bytes 8388608 | tf_op jit(solution)/shard_map/all_to_all | solution.py:116
  28.3 60.3 %scatter_custom_fusion = s32[16384]{0:T(1024)S(1)} fusion(s32[16384]{0:T(1024)S(1)} %compare_select_fusion, s32[16384]{0:T(1024)S(1)} %iota.15, s32[]{:T(128)} %copy.33), kind=kCustom, calls=%fused_computation.91 | custom fusion | bytes 65540 | tf_op jit(solution)/shard_map/scatter | solution.py:120
  103.6 5.3 collective-permute-start.9
  118.2 747.3 %while.11 = (s32[]{:T(128)}, f32[5,128,1024]{2,1,0:T(8,128)}, f32[128,1024]{1,0:T(8,128)S(1)}, f32[132,1028]{1,0:T(8,128)}, f32[128,1024]{1,0:T(8,128)}, /*index...) while((s32[]{:T(128)}, f32[5,128,1024]{2,1,0:T(8,128)}, ...), condition=%wide.region_9.10_spmd.clone, body=%wide.region_8.9_spmd.sunk.clone.sunk | while | flops 10502272 | bytes 61185656 | solution.py:142
  123.1 8.1 collective-permute-done
  168.9 7.6 collective-permute-done
  190.7 4.8 collective-permute-start.2
  214.9 7.9 collective-permute-done
  261.7 6.4 collective-permute-done
  286.2 7.5 collective-permute-start.6
  330.8 10.0 %collective-permute-start.6 = (f32[5,2,1028]{2,1,0:T(2,128)S(1)}, f32[5,2,1028]{2,1,0:T(2,128)S(1)}, u32[]{:S(2)}, u32[]{:S(2)}) collective-permute-start(f32[5,2,1028]{2,1,0:T(2,128)S(1)} %get-tuple-element.175), channel_id=1, source_target_pairs={{0,1},{1,2},{2,3},{3,4},{4,5},{5,6},{6,7},{7,8},{8,9},{9,10},{10,1... | collective-permute-start | bytes 123368 | tf_op jit(solution)/shard_map/while/body/eval_jaxpr/ppermute | solution.py:23
  378.1 10.8 %collective-permute-start.6 = (f32[5,2,1028]{2,1,0:T(2,128)S(1)}, f32[5,2,1028]{2,1,0:T(2,128)S(1)}, u32[]{:S(2)}, u32[]{:S(2)}) collective-permute-start(f32[5,2,1028]{2,1,0:T(2,128)S(1)} %get-tuple-element.175), channel_id=1, source_target_pairs={{0,1},{1,2},{2,3},{3,4},{4,5},{5,6},{6,7},{7,8},{8,9},{9,10},{10,1... | collective-permute-start | bytes 123368 | tf_op jit(solution)/shard_map/while/body/eval_jaxpr/ppermute | solution.py:23
  425.3 10.6 %collective-permute-start.6 = (f32[5,2,1028]{2,1,0:T(2,128)S(1)}, f32[5,2,1028]{2,1,0:T(2,128)S(1)}, u32[]{:S(2)}, u32[]{:S(2)}) collective-permute-start(f32[5,2,1028]{2,1,0:T(2,128)S(1)} %get-tuple-element.175), channel_id=1, source_target_pairs={{0,1},{1,2},{2,3},{3,4},{4,5},{5,6},{6,7},{7,8},{8,9},{9,10},{10,1... | collective-permute-start | bytes 123368 | tf_op jit(solution)/shard_map/while/body/eval_jaxpr/ppermute | solution.py:23
  472.8 10.4 %collective-permute-start.6 = (f32[5,2,1028]{2,1,0:T(2,128)S(1)}, f32[5,2,1028]{2,1,0:T(2,128)S(1)}, u32[]{:S(2)}, u32[]{:S(2)}) collective-permute-start(f32[5,2,1028]{2,1,0:T(2,128)S(1)} %get-tuple-element.175), channel_id=1, source_target_pairs={{0,1},{1,2},{2,3},{3,4},{4,5},{5,6},{6,7},{7,8},{8,9},{9,10},{10,1... | collective-permute-start | bytes 123368 | tf_op jit(solution)/shard_map/while/body/eval_jaxpr/ppermute | solution.py:23
  519.7 9.8 %collective-permute-start.6 = (f32[5,2,1028]{2,1,0:T(2,128)S(1)}, f32[5,2,1028]{2,1,0:T(2,128)S(1)}, u32[]{:S(2)}, u32[]{:S(2)}) collective-permute-start(f32[5,2,1028]{2,1,0:T(2,128)S(1)} %get-tuple-element.175), channel_id=1, source_target_pairs={{0,1},{1,2},{2,3},{3,4},{4,5},{5,6},{6,7},{7,8},{8,9},{9,10},{10,1... | collective-permute-start | bytes 123368 | tf_op jit(solution)/shard_map/while/body/eval_jaxpr/ppermute | solution.py:23
  566.2 8.6 collective-permute-start.6
  611.3 8.4 collective-permute-start.6
  656.3 8.4 collective-permute-start.6
  701.3 10.9 %collective-permute-start.6 = (f32[5,2,1028]{2,1,0:T(2,128)S(1)}, f32[5,2,1028]{2,1,0:T(2,128)S(1)}, u32[]{:S(2)}, u32[]{:S(2)}) collective-permute-start(f32[5,2,1028]{2,1,0:T(2,128)S(1)} %get-tuple-element.175), channel_id=1, source_target_pairs={{0,1},{1,2},{2,3},{3,4},{4,5},{5,6},{6,7},{7,8},{8,9},{9,10},{10,1... | collective-permute-start | bytes 123368 | tf_op jit(solution)/shard_map/while/body/eval_jaxpr/ppermute | solution.py:23
  748.6 10.7 %collective-permute-start.6 = (f32[5,2,1028]{2,1,0:T(2,128)S(1)}, f32[5,2,1028]{2,1,0:T(2,128)S(1)}, u32[]{:S(2)}, u32[]{:S(2)}) collective-permute-start(f32[5,2,1028]{2,1,0:T(2,128)S(1)} %get-tuple-element.175), channel_id=1, source_target_pairs={{0,1},{1,2},{2,3},{3,4},{4,5},{5,6},{6,7},{7,8},{8,9},{9,10},{10,1... | collective-permute-start | bytes 123368 | tf_op jit(solution)/shard_map/while/body/eval_jaxpr/ppermute | solution.py:23
  796.0 11.1 %collective-permute-start.6 = (f32[5,2,1028]{2,1,0:T(2,128)S(1)}, f32[5,2,1028]{2,1,0:T(2,128)S(1)}, u32[]{:S(2)}, u32[]{:S(2)}) collective-permute-start(f32[5,2,1028]{2,1,0:T(2,128)S(1)} %get-tuple-element.175), channel_id=1, source_target_pairs={{0,1},{1,2},{2,3},{3,4},{4,5},{5,6},{6,7},{7,8},{8,9},{9,10},{10,1... | collective-permute-start | bytes 123368 | tf_op jit(solution)/shard_map/while/body/eval_jaxpr/ppermute | solution.py:23
  843.5 10.9 %collective-permute-start.6 = (f32[5,2,1028]{2,1,0:T(2,128)S(1)}, f32[5,2,1028]{2,1,0:T(2,128)S(1)}, u32[]{:S(2)}, u32[]{:S(2)}) collective-permute-start(f32[5,2,1028]{2,1,0:T(2,128)S(1)} %get-tuple-element.175), channel_id=1, source_target_pairs={{0,1},{1,2},{2,3},{3,4},{4,5},{5,6},{6,7},{7,8},{8,9},{9,10},{10,1... | collective-permute-start | bytes 123368 | tf_op jit(solution)/shard_map/while/body/eval_jaxpr/ppermute | solution.py:23
  875.4 29.0 %all-to-all-start.1 = ((f32[256,2,8,128]{3,2,1,0:T(8,128)}), f32[256,2,8,128]{3,2,1,0:T(8,128)}, u32[]{:S(2)}, u32[]{:S(2)}) async-start(f32[256,2,8,128]{3,2,1,0:T(8,128)} %select_select_fusion.1), calls=%async_computation.1 | async-start | bytes 4194304 | tf_op jit(solution)/shard_map/all_to_all | solution.py:150
  907.2 27.3 %all-to-all-done.1 = f32[256,2,8,128]{3,2,1,0:T(8,128)} async-done(((f32[256,2,8,128]{3,2,1,0:T(8,128)}), f32[256,2,8,128]{3,2,1,0:T(8,128)}, u32[]{:S(2)}, u32[]{:S(2)}) %all-to-all-start.1) | async-done | bytes 2097184 | tf_op jit(solution)/shard_map/all_to_all | solution.py:150
  (639 shorter events, 640.3 us)
Async XLA Ops:
  10.0 100.7 %all-to-all-start = ((f32[256,4,8,128]{3,2,1,0:T(8,128)}), f32[256,4,8,128]{3,2,1,0:T(8,128)}, u32[]{:S(2)}, u32[]{:S(2)}) async-start(f32[256,4,8,128]{3,2,1,0:T(8,128)} %select_select_fusion), calls=%async_computation | async-start | bytes 8388608 | tf_op jit(solution)/shard_map/all_to_all | solution.py:116
  23.6 69.8 %collective-permute-start.7 = (f32[1,128,2]{2,1,0:T(8,128)}, f32[1,128,2]{2,1,0:T(8,128)S(1)}, u32[]{:S(2)}, u32[]{:S(2)}) collective-permute-start(f32[1,128,2]{2,1,0:T(8,128)} %get-tuple-element.109), channel_id=1, source_target_pairs={{0,16},{16,32},{32,48},{48,64},{64,80},{80,96},{96,112},{112,0},{1... | collective-permute-start | bytes 3080 | tf_op jit(solution)/shard_map/ppermute | solution.py:23
  25.1 68.3 %collective-permute-start.8 = (f32[1,128,2]{2,1,0:T(8,128)}, f32[1,128,2]{2,1,0:T(8,128)S(1)}, u32[]{:S(2)}, u32[]{:S(2)}) collective-permute-start(f32[1,128,2]{2,1,0:T(8,128)} %get-tuple-element.108), channel_id=1, source_target_pairs={{16,0},{32,16},{48,32},{64,48},{80,64},{96,80},{112,96},{0,112},{1... | collective-permute-start | bytes 3080 | tf_op jit(solution)/shard_map/ppermute | solution.py:24
  327.6 13.2 %collective-permute-start.5 = (f32[5,2,1028]{2,1,0:T(2,128)S(1)}, f32[5,2,1028]{2,1,0:T(2,128)S(1)}, u32[]{:S(2)}, u32[]{:S(2)}) collective-permute-start(f32[5,2,1028]{2,1,0:T(2,128)S(1)} %collective-permute-done.4), channel_id=1, source_target_pairs={{0,64},{16,80},{32,96},{48,112},{64,0},{80,16},{96,32},{112,48},{1... | collective-permute-start | bytes 123368 | tf_op jit(solution)/shard_map/while/body/eval_jaxpr/ppermute | solution.py:30
  328.9 13.0 %collective-permute-start.2 = (f32[5,2,1028]{2,1,0:T(2,128)S(1)}, f32[5,2,1028]{2,1,0:T(2,128)S(1)}, u32[]{:S(2)}, u32[]{:S(2)}) collective-permute-start(f32[5,2,1028]{2,1,0:T(2,128)S(1)} %get-tuple-element.174), channel_id=1, source_target_pairs={{1,0},{2,1},{3,2},{4,3},{5,4},{6,5},{7,6},{8,7},{9,8},{10,9},{11,1... | collective-permute-start | bytes 123368 | tf_op jit(solution)/shard_map/while/body/eval_jaxpr/ppermute | solution.py:24
  375.2 13.7 %collective-permute-start.5 = (f32[5,2,1028]{2,1,0:T(2,128)S(1)}, f32[5,2,1028]{2,1,0:T(2,128)S(1)}, u32[]{:S(2)}, u32[]{:S(2)}) collective-permute-start(f32[5,2,1028]{2,1,0:T(2,128)S(1)} %collective-permute-done.4), channel_id=1, source_target_pairs={{0,64},{16,80},{32,96},{48,112},{64,0},{80,16},{96,32},{112,48},{1... | collective-permute-start | bytes 123368 | tf_op jit(solution)/shard_map/while/body/eval_jaxpr/ppermute | solution.py:30
  376.1 13.7 %collective-permute-start.2 = (f32[5,2,1028]{2,1,0:T(2,128)S(1)}, f32[5,2,1028]{2,1,0:T(2,128)S(1)}, u32[]{:S(2)}, u32[]{:S(2)}) collective-permute-start(f32[5,2,1028]{2,1,0:T(2,128)S(1)} %get-tuple-element.174), channel_id=1, source_target_pairs={{1,0},{2,1},{3,2},{4,3},{5,4},{6,5},{7,6},{8,7},{9,8},{10,9},{11,1... | collective-permute-start | bytes 123368 | tf_op jit(solution)/shard_map/while/body/eval_jaxpr/ppermute | solution.py:24
  422.6 13.3 %collective-permute-start.5 = (f32[5,2,1028]{2,1,0:T(2,128)S(1)}, f32[5,2,1028]{2,1,0:T(2,128)S(1)}, u32[]{:S(2)}, u32[]{:S(2)}) collective-permute-start(f32[5,2,1028]{2,1,0:T(2,128)S(1)} %collective-permute-done.4), channel_id=1, source_target_pairs={{0,64},{16,80},{32,96},{48,112},{64,0},{80,16},{96,32},{112,48},{1... | collective-permute-start | bytes 123368 | tf_op jit(solution)/shard_map/while/body/eval_jaxpr/ppermute | solution.py:30
  423.4 13.5 %collective-permute-start.2 = (f32[5,2,1028]{2,1,0:T(2,128)S(1)}, f32[5,2,1028]{2,1,0:T(2,128)S(1)}, u32[]{:S(2)}, u32[]{:S(2)}) collective-permute-start(f32[5,2,1028]{2,1,0:T(2,128)S(1)} %get-tuple-element.174), channel_id=1, source_target_pairs={{1,0},{2,1},{3,2},{4,3},{5,4},{6,5},{7,6},{8,7},{9,8},{10,9},{11,1... | collective-permute-start | bytes 123368 | tf_op jit(solution)/shard_map/while/body/eval_jaxpr/ppermute | solution.py:24
  470.3 13.0 %collective-permute-start.5 = (f32[5,2,1028]{2,1,0:T(2,128)S(1)}, f32[5,2,1028]{2,1,0:T(2,128)S(1)}, u32[]{:S(2)}, u32[]{:S(2)}) collective-permute-start(f32[5,2,1028]{2,1,0:T(2,128)S(1)} %collective-permute-done.4), channel_id=1, source_target_pairs={{0,64},{16,80},{32,96},{48,112},{64,0},{80,16},{96,32},{112,48},{1... | collective-permute-start | bytes 123368 | tf_op jit(solution)/shard_map/while/body/eval_jaxpr/ppermute | solution.py:30
  470.9 13.4 %collective-permute-start.2 = (f32[5,2,1028]{2,1,0:T(2,128)S(1)}, f32[5,2,1028]{2,1,0:T(2,128)S(1)}, u32[]{:S(2)}, u32[]{:S(2)}) collective-permute-start(f32[5,2,1028]{2,1,0:T(2,128)S(1)} %get-tuple-element.174), channel_id=1, source_target_pairs={{1,0},{2,1},{3,2},{4,3},{5,4},{6,5},{7,6},{8,7},{9,8},{10,9},{11,1... | collective-permute-start | bytes 123368 | tf_op jit(solution)/shard_map/while/body/eval_jaxpr/ppermute | solution.py:24
  517.8 12.7 %collective-permute-start.2 = (f32[5,2,1028]{2,1,0:T(2,128)S(1)}, f32[5,2,1028]{2,1,0:T(2,128)S(1)}, u32[]{:S(2)}, u32[]{:S(2)}) collective-permute-start(f32[5,2,1028]{2,1,0:T(2,128)S(1)} %get-tuple-element.174), channel_id=1, source_target_pairs={{1,0},{2,1},{3,2},{4,3},{5,4},{6,5},{7,6},{8,7},{9,8},{10,9},{11,1... | collective-permute-start | bytes 123368 | tf_op jit(solution)/shard_map/while/body/eval_jaxpr/ppermute | solution.py:24
  698.6 13.6 %collective-permute-start.5 = (f32[5,2,1028]{2,1,0:T(2,128)S(1)}, f32[5,2,1028]{2,1,0:T(2,128)S(1)}, u32[]{:S(2)}, u32[]{:S(2)}) collective-permute-start(f32[5,2,1028]{2,1,0:T(2,128)S(1)} %collective-permute-done.4), channel_id=1, source_target_pairs={{0,64},{16,80},{32,96},{48,112},{64,0},{80,16},{96,32},{112,48},{1... | collective-permute-start | bytes 123368 | tf_op jit(solution)/shard_map/while/body/eval_jaxpr/ppermute | solution.py:30
  699.3 13.8 %collective-permute-start.2 = (f32[5,2,1028]{2,1,0:T(2,128)S(1)}, f32[5,2,1028]{2,1,0:T(2,128)S(1)}, u32[]{:S(2)}, u32[]{:S(2)}) collective-permute-start(f32[5,2,1028]{2,1,0:T(2,128)S(1)} %get-tuple-element.174), channel_id=1, source_target_pairs={{1,0},{2,1},{3,2},{4,3},{5,4},{6,5},{7,6},{8,7},{9,8},{10,9},{11,1... | collective-permute-start | bytes 123368 | tf_op jit(solution)/shard_map/while/body/eval_jaxpr/ppermute | solution.py:24
  701.3 12.0 %collective-permute-start.6 = (f32[5,2,1028]{2,1,0:T(2,128)S(1)}, f32[5,2,1028]{2,1,0:T(2,128)S(1)}, u32[]{:S(2)}, u32[]{:S(2)}) collective-permute-start(f32[5,2,1028]{2,1,0:T(2,128)S(1)} %get-tuple-element.175), channel_id=1, source_target_pairs={{0,1},{1,2},{2,3},{3,4},{4,5},{5,6},{6,7},{7,8},{8,9},{9,10},{10,1... | collective-permute-start | bytes 123368 | tf_op jit(solution)/shard_map/while/body/eval_jaxpr/ppermute | solution.py:23
  745.9 13.4 %collective-permute-start.5 = (f32[5,2,1028]{2,1,0:T(2,128)S(1)}, f32[5,2,1028]{2,1,0:T(2,128)S(1)}, u32[]{:S(2)}, u32[]{:S(2)}) collective-permute-start(f32[5,2,1028]{2,1,0:T(2,128)S(1)} %collective-permute-done.4), channel_id=1, source_target_pairs={{0,64},{16,80},{32,96},{48,112},{64,0},{80,16},{96,32},{112,48},{1... | collective-permute-start | bytes 123368 | tf_op jit(solution)/shard_map/while/body/eval_jaxpr/ppermute | solution.py:30
  746.7 13.6 %collective-permute-start.2 = (f32[5,2,1028]{2,1,0:T(2,128)S(1)}, f32[5,2,1028]{2,1,0:T(2,128)S(1)}, u32[]{:S(2)}, u32[]{:S(2)}) collective-permute-start(f32[5,2,1028]{2,1,0:T(2,128)S(1)} %get-tuple-element.174), channel_id=1, source_target_pairs={{1,0},{2,1},{3,2},{4,3},{5,4},{6,5},{7,6},{8,7},{9,8},{10,9},{11,1... | collective-permute-start | bytes 123368 | tf_op jit(solution)/shard_map/while/body/eval_jaxpr/ppermute | solution.py:24
  793.4 13.7 %collective-permute-start.5 = (f32[5,2,1028]{2,1,0:T(2,128)S(1)}, f32[5,2,1028]{2,1,0:T(2,128)S(1)}, u32[]{:S(2)}, u32[]{:S(2)}) collective-permute-start(f32[5,2,1028]{2,1,0:T(2,128)S(1)} %collective-permute-done.4), channel_id=1, source_target_pairs={{0,64},{16,80},{32,96},{48,112},{64,0},{80,16},{96,32},{112,48},{1... | collective-permute-start | bytes 123368 | tf_op jit(solution)/shard_map/while/body/eval_jaxpr/ppermute | solution.py:30
  794.0 14.0 %collective-permute-start.2 = (f32[5,2,1028]{2,1,0:T(2,128)S(1)}, f32[5,2,1028]{2,1,0:T(2,128)S(1)}, u32[]{:S(2)}, u32[]{:S(2)}) collective-permute-start(f32[5,2,1028]{2,1,0:T(2,128)S(1)} %get-tuple-element.174), channel_id=1, source_target_pairs={{1,0},{2,1},{3,2},{4,3},{5,4},{6,5},{7,6},{8,7},{9,8},{10,9},{11,1... | collective-permute-start | bytes 123368 | tf_op jit(solution)/shard_map/while/body/eval_jaxpr/ppermute | solution.py:24
  796.0 12.2 %collective-permute-start.6 = (f32[5,2,1028]{2,1,0:T(2,128)S(1)}, f32[5,2,1028]{2,1,0:T(2,128)S(1)}, u32[]{:S(2)}, u32[]{:S(2)}) collective-permute-start(f32[5,2,1028]{2,1,0:T(2,128)S(1)} %get-tuple-element.175), channel_id=1, source_target_pairs={{0,1},{1,2},{2,3},{3,4},{4,5},{5,6},{6,7},{7,8},{8,9},{9,10},{10,1... | collective-permute-start | bytes 123368 | tf_op jit(solution)/shard_map/while/body/eval_jaxpr/ppermute | solution.py:23
  841.0 13.5 %collective-permute-start.5 = (f32[5,2,1028]{2,1,0:T(2,128)S(1)}, f32[5,2,1028]{2,1,0:T(2,128)S(1)}, u32[]{:S(2)}, u32[]{:S(2)}) collective-permute-start(f32[5,2,1028]{2,1,0:T(2,128)S(1)} %collective-permute-done.4), channel_id=1, source_target_pairs={{0,64},{16,80},{32,96},{48,112},{64,0},{80,16},{96,32},{112,48},{1... | collective-permute-start | bytes 123368 | tf_op jit(solution)/shard_map/while/body/eval_jaxpr/ppermute | solution.py:30
  841.6 13.9 %collective-permute-start.2 = (f32[5,2,1028]{2,1,0:T(2,128)S(1)}, f32[5,2,1028]{2,1,0:T(2,128)S(1)}, u32[]{:S(2)}, u32[]{:S(2)}) collective-permute-start(f32[5,2,1028]{2,1,0:T(2,128)S(1)} %get-tuple-element.174), channel_id=1, source_target_pairs={{1,0},{2,1},{3,2},{4,3},{5,4},{6,5},{7,6},{8,7},{9,8},{10,9},{11,1... | collective-permute-start | bytes 123368 | tf_op jit(solution)/shard_map/while/body/eval_jaxpr/ppermute | solution.py:24
  843.5 12.1 %collective-permute-start.6 = (f32[5,2,1028]{2,1,0:T(2,128)S(1)}, f32[5,2,1028]{2,1,0:T(2,128)S(1)}, u32[]{:S(2)}, u32[]{:S(2)}) collective-permute-start(f32[5,2,1028]{2,1,0:T(2,128)S(1)} %get-tuple-element.175), channel_id=1, source_target_pairs={{0,1},{1,2},{2,3},{3,4},{4,5},{5,6},{6,7},{7,8},{8,9},{9,10},{10,1... | collective-permute-start | bytes 123368 | tf_op jit(solution)/shard_map/while/body/eval_jaxpr/ppermute | solution.py:23
  875.4 59.1 %all-to-all-start.1 = ((f32[256,2,8,128]{3,2,1,0:T(8,128)}), f32[256,2,8,128]{3,2,1,0:T(8,128)}, u32[]{:S(2)}, u32[]{:S(2)}) async-start(f32[256,2,8,128]{3,2,1,0:T(8,128)} %select_select_fusion.1), calls=%async_computation.1 | async-start | bytes 4194304 | tf_op jit(solution)/shard_map/all_to_all | solution.py:150
  (168 other events, 838.7 us)
where the time goes:
time: 945 us; the launch traced here: 940 us
  starting transfers between devices  368 us (39%)
  local copies, waits for them, and re-layouts  275 us (29%)
  waiting for transfers between devices  179 us (19%)
  other arithmetic  115 us (12%)
    ppermute x34, starting transfers between devices, padded(): before = lax.ppermute(last, axis, up)  158 us
    ppermute x34, starting transfers between devices, padded(): after = lax.ppermute(leading, axis, down)  98.2 us
    ppermute x34, waiting for transfers between devices, padded(): before = lax.ppermute(last, axis, up)  82.8 us
    while x176, local copies, waits for them, and re-layouts  75.2 us
    concatenate x17, local copies, waits for them, and re-layouts, padded(): shard = jnp.concatenate([before, shard, after], axis=dim)  74 us
    ppermute x51, starting transfers between devices, from_partner(): lax.ppermute(shard, axis, [(i, i ^ 1 << apart) for i in range(lax.axis_si...  70.8 us
    ppermute x51, waiting for transfers between devices, from_partner(): lax.ppermute(shard, axis, [(i, i ^ 1 << apart) for i in range(lax.axis_si...  68.8 us
    scatter x1, local copies, waits for them, and re-layouts, local(): anchor = jnp.zeros((blocks * per_block,), jnp.int32).at[route].set(jnp.ar...  60.3 us
  transfers between devices with their start and end apart: 121, of which 50 were waited for; matrix products, arithmetic and copies ran while one was open for 10% of the time, Pallas kernels for 0%

commit v1 on v0

v1 whole, which is shorter than its diff:
```python
import functools

import jax
import jax.numpy as jnp
from jax import lax
from jax.experimental import pallas as pl
from jax.experimental.pallas import tpu as pltpu
from jax.sharding import PartitionSpec as P

MESH = pl.DeviceIdType.MESH
ITERS = 16
RELAX = 0.1
DRAG = 0.5
TURN = 0.3
TILT = 0.05
KEEP = 1.0 / (1.0 + RELAX)

N_GX = 8
N_GY = 16
N_DEV = 128
HALO = 2 * ITERS
ROWS = 128
EXT = ROWS + 2 * HALO
STEP = EXT // 8
TILES_X = 8
CT = TILES_X + 1

MASS, STRENGTH, ZONAL, MERID, SUM, DIFF, SHEAR, FORCE_X, FORCE_Y = range(9)
STATIC = 7
CU, CV, CXX, CYY, CSH, CSTR = range(6)
KS, KM, KFX, KFY, KA, KB = range(6)


def peers():
    order = []
    for n in range(32):
        j = (n * 13) % 32
        dx, dy, dc = j // 8, (j // 2) % 4, j % 2
        off = (n + n // 4 + 3 * dx + dy) % 4 if (dx, dy, dc) != (0, 0, 0) else 0
        order.append((dx, dy, dc, off))
    return order


def each_peer(visit):
    gx = lax.axis_index("gx")
    gy = lax.axis_index("gy")
    z, x_lo = gx % 4, gx // 4
    x_hi, y, core = gy // 8, (gy // 2) % 4, gy % 2
    x = x_hi * 2 + x_lo
    xs = [(x + d) % 4 for d in range(4)]
    part_gx = [(v % 2) * 4 for v in xs]
    part_gy = [(v // 2) * 8 for v in xs]
    ys = [((y + d) % 4) * 2 for d in range(4)]
    cores = [core, 1 - core]
    zs = tuple((z + d) % 4 for d in range(4))

    def turn(q, zs):
        for dx, dy, dc, off in peers():
            there = (part_gx[dx] + zs[off], part_gy[dx] + ys[dy] + cores[dc])
            if (dx, dy, dc) == (0, 0, 0):
                pl.when(q > 0)(functools.partial(visit, *there))
            else:
                visit(*there)
        return zs[1:] + zs[:1]

    lax.fori_loop(0, 4, turn, zs)


def wait_for(ref, sem):
    pltpu.make_async_copy(ref, ref, sem).wait()


def left_right(row, lane):
    n = len(row)
    left = [pltpu.roll(jnp.where(lane == 127, row[j - 1], row[j]), 1, 1) for j in range(n)]
    right = [pltpu.roll(jnp.where(lane == 0, row[(j + 1) % n], row[j]), 127, 1) for j in range(n)]
    return left, right


def kernel(
    send_tile, recv_slot, back_tile, back_slot,
    ocean, mask, mass, strength, velocity, stress,
    out_velocity, out_stress,
    tiles, returning, arrived_back, oc, outgoing, arrived, ext, ext_mask, side_w, side_e, mask_w, mask_e, side_fw, side_fe,
    state, const, in_sem, a2a_sem, halo_sem,
):
    gx = lax.axis_index("gx")
    gy = lax.axis_index("gy")
    me = gx * N_GY + gy
    top = gy == N_GY - 1
    inner = pl.ds(HALO, ROWS)
    lane = lax.broadcasted_iota(jnp.int32, (8, 128), 1)

    pltpu.make_async_copy(ocean, oc, in_sem.at[0]).start()
    for j in range(TILES_X):
        cols = pl.ds(j * 128, 128)
        pltpu.make_async_copy(mass.at[:, cols], ext.at[MASS, j, inner], in_sem.at[1]).start()
        pltpu.make_async_copy(strength.at[:, cols], ext.at[STRENGTH, j, inner], in_sem.at[1]).start()
        pltpu.make_async_copy(velocity.at[:, :, cols], ext.at[pl.ds(ZONAL, 2), j, inner], in_sem.at[1]).start()
        pltpu.make_async_copy(stress.at[:, :, cols], ext.at[pl.ds(SUM, 3), j, inner], in_sem.at[1]).start()
        pltpu.make_async_copy(mask.at[:, cols], ext_mask.at[j, inner], in_sem.at[2]).start()

    barrier = pltpu.get_barrier_semaphore()

    def greet(a, b):
        pl.semaphore_signal(barrier, inc=1, device_id=(a, b), device_id_type=MESH)

    each_peer(greet)

    wait_for(oc, in_sem.at[0])

    def pack(i, carry):
        for h in range(8):
            outgoing[i * 8 + h] = oc[send_tile[i * 8 + h]]
        return carry

    lax.fori_loop(0, 2 * N_DEV // 8, pack, 0)
    pl.semaphore_wait(barrier, N_DEV - 1)

    def send_forcing(a, b):
        pltpu.make_async_remote_copy(
            outgoing.at[pl.ds((a * N_GY + b) * 2, 2)], arrived.at[pl.ds(me * 2, 2)],
            a2a_sem.at[0], a2a_sem.at[1], device_id=(a, b), device_id_type=MESH,
        ).start()

    wait_for(ext.at[pl.ds(0, STATIC), pl.ds(0, TILES_X), inner], in_sem.at[1])
    wait_for(ext_mask.at[pl.ds(0, TILES_X), inner], in_sem.at[2])
    east = ((gx + 1) % N_GX, gy)
    west = ((gx + N_GX - 1) % N_GX, gy)

    def columns(first, count, to_west, to_east, sems):
        a = pltpu.make_async_remote_copy(
            ext.at[pl.ds(first, count), TILES_X - 1, inner], to_west,
            halo_sem.at[sems], halo_sem.at[sems + 1], device_id=east, device_id_type=MESH)
        b = pltpu.make_async_remote_copy(
            ext.at[pl.ds(first, count), 0, inner], to_east,
            halo_sem.at[sems + 2], halo_sem.at[sems + 3], device_id=west, device_id_type=MESH)
        return a, b

    def mask_columns(sems):
        a = pltpu.make_async_remote_copy(
            ext_mask.at[TILES_X - 1, inner], mask_w,
            halo_sem.at[sems], halo_sem.at[sems + 1], device_id=east, device_id_type=MESH)
        b = pltpu.make_async_remote_copy(
            ext_mask.at[0, inner], mask_e,
            halo_sem.at[sems + 2], halo_sem.at[sems + 3], device_id=west, device_id_type=MESH)
        return a, b

    def merge(first, count, from_west, from_east):
        def body(i, carry):
            rows = pl.ds(pl.multiple_of(i * 8, 8), 8)
            there = pl.ds(pl.multiple_of(HALO + i * 8, 8), 8)
            for f in range(count):
                ext[first + f, TILES_X, there] = jnp.where(lane < 64, from_east[f, rows], from_west[f, rows])
            return carry
        lax.fori_loop(0, ROWS // 8, body, 0)

    north_gy = jnp.minimum(gy + 1, N_GY - 1)
    south_gy = jnp.maximum(gy - 1, 0)

    def rows_start(ref, sems):
        to_north = pltpu.make_async_remote_copy(
            ref(pl.ds(ROWS, HALO)), ref(pl.ds(0, HALO)),
            halo_sem.at[sems], halo_sem.at[sems + 1], device_id=(gx, north_gy), device_id_type=MESH)
        to_partner = pltpu.make_async_remote_copy(
            ref(pl.ds(ROWS, HALO)), ref(pl.ds(HALO + ROWS, HALO)),
            halo_sem.at[sems], halo_sem.at[sems + 3], device_id=(N_GX - 1 - gx, gy), device_id_type=MESH)
        to_south = pltpu.make_async_remote_copy(
            ref(pl.ds(HALO, HALO)), ref(pl.ds(HALO + ROWS, HALO)),
            halo_sem.at[sems + 2], halo_sem.at[sems + 3], device_id=(gx, south_gy), device_id_type=MESH)
        pl.when(jnp.logical_not(top))(to_north.start)
        pl.when(top)(to_partner.start)
        pl.when(gy > 0)(to_south.start)

    def rows_wait(ref, sems):
        wait_for(ref(pl.ds(HALO + ROWS, HALO)), halo_sem.at[sems + 3])
        wait_for(ref(pl.ds(ROWS, HALO)), halo_sem.at[sems])

        @pl.when(gy > 0)
        def _():
            wait_for(ref(pl.ds(0, HALO)), halo_sem.at[sems + 1])
            wait_for(ref(pl.ds(HALO, HALO)), halo_sem.at[sems + 2])

    def static_ref(rows):
        return ext.at[pl.ds(0, STATIC), :, rows]

    def mask_ref(rows):
        return ext_mask.at[:, rows]

    def force_ref(rows):
        return ext.at[pl.ds(FORCE_X, 2), :, rows]

    back_sub = 7 - lax.broadcasted_iota(jnp.int32, (8, 128), 0)
    back_lane = 127 - lane

    def turned(x):
        x = jnp.take_along_axis(x, back_lane, axis=1)
        return jnp.take_along_axis(x, back_sub, axis=0)

    def fold(get, put):
        def body(p, carry):
            here = pl.ds(pl.multiple_of(HALO + ROWS + p * 8, 8), 8)
            there = pl.ds(pl.multiple_of(HALO + ROWS + HALO - 8 - p * 8, 8), 8)
            for j in range(TILES_X // 2):
                a, b = get(j, here), get(TILES_X - 1 - j, there)
                put(j, here, turned(b))
                put(TILES_X - 1 - j, there, turned(a))
            return carry
        lax.fori_loop(0, HALO // 8, body, 0)

        def last(p, carry):
            here = pl.ds(pl.multiple_of(HALO + ROWS + p * 8, 8), 8)
            there = pl.ds(pl.multiple_of(HALO + ROWS + HALO - 8 - p * 8, 8), 8)
            a, b = get(TILES_X, here), get(TILES_X, there)
            put(TILES_X, here, turned(b))
            put(TILES_X, there, turned(a))
            return carry
        lax.fori_loop(0, HALO // 16, last, 0)

    def fold_field(f, sign):
        def put(j, rows, x):
            ext[f, j, rows] = x * sign
        fold(lambda j, rows: ext[f, j, rows], put)

    def fold_mask():
        def put(j, rows, x):
            ext_mask[j, rows] = x
        fold(lambda j, rows: ext_mask[j, rows], put)

    static_cols = columns(0, STATIC, side_w, side_e, 0)
    mask_cols = mask_columns(4)
    for copy in static_cols + mask_cols:
        copy.start()
    each_peer(send_forcing)
    for h in range(2):
        arrived[me * 2 + h] = outgoing[me * 2 + h]
    for copy in static_cols + mask_cols:
        copy.wait()
    merge(0, STATIC, side_w, side_e)

    def merge_mask(i, carry):
        rows = pl.ds(pl.multiple_of(i * 8, 8), 8)
        there = pl.ds(pl.multiple_of(HALO + i * 8, 8), 8)
        ext_mask[TILES_X, there] = jnp.where(lane < 64, mask_e[rows], mask_w[rows])
        return carry

    lax.fori_loop(0, ROWS // 8, merge_mask, 0)
    rows_start(static_ref, 8)
    rows_start(mask_ref, 12)

    @pl.when(gy == 0)
    def _():
        zero = jnp.zeros((8, 128), jnp.float32)
        for p in range(HALO // 8):
            rows = pl.ds(p * 8, 8)

            def clear(j, carry):
                for f in range(9):
                    ext[f, j, rows] = zero + 1.0 if f == MASS else zero
                ext_mask[j, rows] = jnp.zeros((8, 128), jnp.int32)
                return carry

            lax.fori_loop(0, CT, clear, 0)

    rows_wait(static_ref, 8)
    rows_wait(mask_ref, 12)

    @pl.when(top)
    def _():
        for f in range(STATIC):
            fold_field(f, -1.0 if f in (ZONAL, MERID) else 1.0)
        fold_mask()

    def arrange(r, carry):
        rows = pl.ds(r, 8, stride=STEP)
        for j in range(CT):
            share = ext_mask[j, rows].astype(jnp.float32)
            m = ext[MASS, j, rows]
            strong = ext[STRENGTH, j, rows]
            a = m + DRAG
            b = TURN * m
            scale = share / (a * a + b * b)
            const[KM, r, j] = m
            const[KA, r, j] = a * scale
            const[KB, r, j] = b * scale
            const[KS, r, j] = (0.0125 * KEEP) * strong
            state[CSTR, r + 1, j] = strong
            state[CU, r + 1, j] = ext[ZONAL, j, rows] * share
            state[CV, r + 1, j] = ext[MERID, j, rows] * share
            both = 0.25 * (ext[SUM, j, rows] + strong)
            apart = 0.25 * ext[DIFF, j, rows]
            state[CXX, r + 1, j] = both + apart
            state[CYY, r + 1, j] = both - apart
            state[CSH, r + 1, j] = 0.5 * ext[SHEAR, j, rows]
        return carry

    lax.fori_loop(0, STEP, arrange, 0)

    def ghosts(names):
        for c in names:
            for j in range(CT):
                state[c, 0, j] = pltpu.roll(state[c, STEP, j], 1, 0)
                state[c, STEP + 1, j] = pltpu.roll(state[c, 1, j], 7, 0)

    ghosts((CU, CV, CSTR))

    wait_for(arrived.at[pl.ds(0, 2 * N_DEV - 2)], a2a_sem.at[1])
    wait_for(outgoing.at[pl.ds(0, 2 * N_DEV - 2)], a2a_sem.at[0])

    def forces(i, carry):
        rows = pl.ds(pl.multiple_of(HALO + i * 8, 8), 8)
        for j in range(TILES_X):
            tile = arrived[recv_slot[i * TILES_X + j]]
            m = TILT * ext[MASS, j, rows]
            ext[FORCE_X, j, rows] = tile[0] + m * tile[2]
            ext[FORCE_Y, j, rows] = tile[1] + m * tile[3]
        return carry

    lax.fori_loop(0, ROWS // 8, forces, 0)
    force_cols = columns(FORCE_X, 2, side_fw, side_fe, 16)
    for copy in force_cols:
        copy.start()
    for copy in force_cols:
        copy.wait()
    merge(FORCE_X, 2, side_fw, side_fe)
    rows_start(force_ref, 20)
    rows_wait(force_ref, 20)

    @pl.when(top)
    def _():
        fold_field(FORCE_X, -1.0)
        fold_field(FORCE_Y, -1.0)

    def arrange_forces(r, carry):
        rows = pl.ds(r, 8, stride=STEP)
        left, right = left_right([state[CSTR, r + 1, j] for j in range(CT)], lane)
        for j in range(CT):
            const[KFX, r, j] = ext[FORCE_X, j, rows] - 0.25 * (right[j] - left[j])
            const[KFY, r, j] = ext[FORCE_Y, j, rows] - 0.25 * (state[CSTR, r + 2, j] - state[CSTR, r, j])
        return carry

    lax.fori_loop(0, STEP, arrange_forces, 0)

    def stresses(r, carry):
        u_left, u_right = left_right([state[CU, r + 1, j] for j in range(CT)], lane)
        v_left, v_right = left_right([state[CV, r + 1, j] for j in range(CT)], lane)
        for j in range(CT):
            ux = u_right[j] - u_left[j]
            vx = v_right[j] - v_left[j]
            uy = state[CU, r + 2, j] - state[CU, r, j]
            vy = state[CV, r + 2, j] - state[CV, r, j]
            div = ux + vy
            ten = ux - vy
            shr = uy + vx
            div2 = div + div
            w = const[KS, r, j] * lax.rsqrt(div2 * div2 + ten * ten + shr * shr + 16.0)
            div4 = div2 + div2
            state[CXX, r + 1, j] = KEEP * state[CXX, r + 1, j] + w * (div4 + ten)
            state[CYY, r + 1, j] = KEEP * state[CYY, r + 1, j] + w * (div4 - ten)
            state[CSH, r + 1, j] = KEEP * state[CSH, r + 1, j] + w * shr
        return carry

    def momentum(r, carry):
        xx_left, xx_right = left_right([state[CXX, r + 1, j] for j in range(CT)], lane)
        sh_left, sh_right = left_right([state[CSH, r + 1, j] for j in range(CT)], lane)
        for j in range(CT):
            px = (xx_right[j] - xx_left[j]) + (state[CSH, r + 2, j] - state[CSH, r, j])
            py = (sh_right[j] - sh_left[j]) + (state[CYY, r + 2, j] - state[CYY, r, j])
            m = const[KM, r, j]
            rx = m * state[CU, r + 1, j] + (px + const[KFX, r, j])
            ry = m * state[CV, r + 1, j] + (py + const[KFY, r, j])
            a = const[KA, r, j]
            b = const[KB, r, j]
            state[CU, r + 1, j] = a * rx + b * ry
            state[CV, r + 1, j] = a * ry - b * rx
        return carry

    def subcycle(t, carry):
        lax.fori_loop(0, STEP, stresses, 0)
        ghosts((CYY, CSH))
        lax.fori_loop(0, STEP, momentum, 0)
        ghosts((CU, CV))
        return carry

    lax.fori_loop(0, ITERS, subcycle, 0)

    def restore(r, carry):
        rows = pl.ds(r, 8, stride=STEP)
        for j in range(TILES_X):
            ext[ZONAL, j, rows] = state[CU, r + 1, j]
            ext[MERID, j, rows] = state[CV, r + 1, j]
            xx = state[CXX, r + 1, j]
            yy = state[CYY, r + 1, j]
            ext[SUM, j, rows] = 2.0 * (xx + yy) - state[CSTR, r + 1, j]
            ext[DIFF, j, rows] = 2.0 * (xx - yy)
            ext[SHEAR, j, rows] = 2.0 * state[CSH, r + 1, j]
        return carry

    lax.fori_loop(0, STEP, restore, 0)
    for j in range(TILES_X):
        cols = pl.ds(j * 128, 128)
        pltpu.make_async_copy(ext.at[pl.ds(SUM, 3), j, inner], out_stress.at[:, :, cols], in_sem.at[1]).start()

    def to_tiles(i, carry):
        rows = pl.ds(pl.multiple_of(HALO + i * 8, 8), 8)
        for j in range(TILES_X):
            tiles[i * TILES_X + j, 0] = ext[ZONAL, j, rows]
            tiles[i * TILES_X + j, 1] = ext[MERID, j, rows]
        return carry

    lax.fori_loop(0, ROWS // 8, to_tiles, 0)

    def pack_back(i, carry):
        for h in range(8):
            returning[i * 8 + h] = tiles[back_tile[i * 8 + h]]
        return carry

    lax.fori_loop(0, 2 * N_DEV // 8, pack_back, 0)

    def send_back(a, b):
        pltpu.make_async_remote_copy(
            returning.at[pl.ds((a * N_GY + b) * 2, 2)], arrived_back.at[pl.ds(me * 2, 2)],
            a2a_sem.at[2], a2a_sem.at[3], device_id=(a, b), device_id_type=MESH,
        ).start()

    each_peer(send_back)
    for h in range(2):
        arrived_back[me * 2 + h] = returning[me * 2 + h]
    wait_for(arrived_back.at[pl.ds(0, 2 * N_DEV - 2)], a2a_sem.at[3])
    wait_for(arrived_back.at[pl.ds(0, 2 * N_DEV - 2)], a2a_sem.at[2])

    def unpack(i, carry):
        for h in range(8):
            out_velocity[i * 8 + h] = arrived_back[back_slot[i * 8 + h]]
        return carry

    lax.fori_loop(0, N_DEV // 8, unpack, 0)
    wait_for(ext.at[pl.ds(SUM, 3), pl.ds(0, TILES_X), inner], in_sem.at[1])


def tables(route):
    me = lax.axis_index("gx") * N_GY + lax.axis_index("gy")
    table = route.reshape(N_DEV, N_DEV)
    number = jnp.arange(N_DEV, dtype=jnp.int32)
    mine = lax.dynamic_index_in_dim(table, me, 0, keepdims=False) // N_DEV
    hits = mine[None, :] == number[:, None]
    first = jnp.min(jnp.where(hits, number[None, :], N_DEV - 1), axis=1)
    second = jnp.max(jnp.where(hits, number[None, :], 0), axis=1)
    send_tile = jnp.stack([first, second], axis=1).reshape(-1)
    rank = jnp.sum(jnp.where(hits & (second[:, None] == number[None, :]), 1, 0), axis=0)
    back_slot = mine * 2 + rank
    here = table // N_DEV == me
    early = jnp.min(jnp.where(here, number[None, :], N_DEV), axis=1)
    late = jnp.max(jnp.where(here, number[None, :], -1), axis=1)
    inside = table % N_DEV
    k_early = jnp.sum(jnp.where(number[None, :] == early[:, None], inside + 1, 0), axis=1) - 1
    k_late = jnp.sum(jnp.where(number[None, :] == late[:, None], inside + 1, 0), axis=1) - 1
    recv_slot = jnp.sum(
        jnp.where(k_early[None, :] == number[:, None], 2 * number[None, :], 0)
        + jnp.where(k_late[None, :] == number[:, None], 2 * number[None, :] + 1, 0), axis=1)
    back_tile = jnp.maximum(jnp.stack([k_early, k_late], axis=1).reshape(-1), 0)
    return send_tile, recv_slot, back_tile, back_slot


def local(ocean_forcing, route, land_mask, mass, strength, velocity_start, stress_start):
    send_tile, recv_slot, back_tile, back_slot = tables(route)
    f32 = jnp.float32
    smem = pl.BlockSpec(memory_space=pltpu.SMEM)
    hbm = pl.BlockSpec(memory_space=pl.ANY)
    return pl.pallas_call(
        kernel,
        out_shape=(
            jax.ShapeDtypeStruct((N_DEV, 2, 8, 128), f32),
            jax.ShapeDtypeStruct((3, ROWS, TILES_X * 128), f32),
        ),
        in_specs=[smem] * 4 + [hbm] * 6,
        out_specs=(pl.BlockSpec(memory_space=pltpu.VMEM), hbm),
        scratch_shapes=[
            pltpu.VMEM((N_DEV, 2, 8, 128), f32),
            pltpu.VMEM((2 * N_DEV, 2, 8, 128), f32),
            pltpu.VMEM((2 * N_DEV, 2, 8, 128), f32),
            pltpu.VMEM((N_DEV, 4, 8, 128), f32),
            pltpu.VMEM((2 * N_DEV, 4, 8, 128), f32),
            pltpu.VMEM((2 * N_DEV, 4, 8, 128), f32),
            pltpu.VMEM((9, CT, EXT, 128), f32),
            pltpu.VMEM((CT, EXT, 128), jnp.int32),
            pltpu.VMEM((STATIC, ROWS, 128), f32),
            pltpu.VMEM((STATIC, ROWS, 128), f32),
            pltpu.VMEM((ROWS, 128), jnp.int32),
            pltpu.VMEM((ROWS, 128), jnp.int32),
            pltpu.VMEM((2, ROWS, 128), f32),
            pltpu.VMEM((2, ROWS, 128), f32),
            pltpu.VMEM((6, STEP + 2, CT, 8, 128), f32),
            pltpu.VMEM((6, STEP, CT, 8, 128), f32),
            pltpu.SemaphoreType.DMA((3,)),
            pltpu.SemaphoreType.DMA((4,)),
            pltpu.SemaphoreType.DMA((24,)),
        ],
        compiler_params=pltpu.CompilerParams(
            collective_id=0, has_side_effects=True, vmem_limit_bytes=56 * 1024 * 1024),
    )(send_tile, recv_slot, back_tile, back_slot, ocean_forcing, land_mask, mass, strength, velocity_start, stress_start)


def solution(mesh):
    placed = (
        P(("gx", "gy"), None, None, None),
        P(),
        P("gy", "gx"),
        P("gy", "gx"),
        P("gy", "gx"),
        P(None, "gy", "gx"),
        P(None, "gy", "gx"),
    )
    return jax.shard_map(
        local,
        mesh=mesh,
        in_specs=placed,
        out_specs=(P(("gx", "gy"), None, None, None), P(None, "gy", "gx")),
        check_vma=False,
    )
```

time: 945 us -> 256 us (0.27)
  starting transfers between devices: 368 us -> 0 us
  local copies, waits for them, and re-layouts: 275 us -> 5.16 us
  Pallas kernels: 0 us -> 245 us
  waiting for transfers between devices: 179 us -> 0 us
  other arithmetic: 115 us -> 4.89 us
    ppermute x119 -> x0, starting transfers between devices: 327 us -> none  [the longest x34 158 us: padded(): before = lax.ppermute(last, axis, up)]
    pallas_call x0 -> x1, Pallas kernels: none -> 245 us  [local(): pl.pallas_call(kernel, out_shape=(jax.ShapeDtypeStruct((N_DEV, 2, 8, 128)...]
    ppermute x119 -> x0, waiting for transfers between devices: 152 us -> none  [the longest x34 82.8 us: padded(): before = lax.ppermute(last, axis, up)]
    while x176 -> x0, local copies, waits for them, and re-layouts: 75.2 us -> none
    concatenate x17 -> x0, local copies, waits for them, and re-layouts: 74 us -> none  [padded(): shard = jnp.concatenate([before, shard, after], axis=dim)]
    scatter x1 -> x0, local copies, waits for them, and re-layouts: 60.3 us -> none  [local(): anchor = jnp.zeros((blocks * per_block,), jnp.int32).at[route].set(jnp.ar...]
    slice x36 -> x0, local copies, waits for them, and re-layouts: 42.9 us -> none  [the longest x18 21.2 us: padded(): leading = lax.slice_in_dim(shard, 0, width, axis=dim)]
    all_to_all x2 -> x0, starting transfers between devices: 40.9 us -> none  [the longest x1 29 us: local(): lax.all_to_all(returning, ('gx', 'gy'), split_axis=0, concat_axis=0, tile...]
  transfers between devices with their start and end apart: 121 -> 0, of which waited for: 50 -> 0; matrix products, arithmetic and copies ran while one was open for 10% -> 0% of each run, Pallas kernels for 0% -> 0%
where the time goes in v1:
time: 256 us
  Pallas kernels  245 us (96%)
  local copies, waits for them, and re-layouts  5.16 us (2%)
  other arithmetic  4.89 us (2%)
    pallas_call x1, Pallas kernels, local(): pl.pallas_call(kernel, out_shape=(jax.ShapeDtypeStruct((N_DEV, 2, 8, 128)...  245 us

profile of v1, /device:TPU:1, one launch (start us, length us, event | category | flops | bytes accessed | tf_op | source)
XLA Modules:
  0.0 255.8 jit_solution(12674269439655635491)
XLA Ops:
  0.6 0.7 fusion.5
  1.3 0.1 select_reduce_fusion.5
  1.5 0.1 select_reduce_fusion
  1.6 1.3 multiply_add_fusion.back_slot
  2.9 1.0 select_reduce_fusion.4
  3.9 1.0 select_reduce_fusion.3
  4.9 0.6 add_reduce_fusion.recv_slot
  5.6 0.1 copy.10
  5.7 0.7 max.10.back_tile
  6.4 0.1 copy.9
  6.5 0.7 reshape.49.send_tile
  7.2 245.1 %shard_map.86 = (f32[128,2,8,128]{3,2,1,0:T(8,128)}, f32[3,128,1024]{2,1,0:T(8,128)}) custom-call(s32[256]{0:T(256)} %reshape.49.send_tile, s32[128]{0:T(128)} %add_reduce_fusion.recv_slot, s32[256]{0:T(256)} %max.10.back_tile, s32[128]{0:T(128)} %multiply_add_fusion.back_slot, f32[128,4,8,128]{3,2,1,0:T(8,128)} %ocean.1, s32[128,1024]{1,0:T(8,128)} %mask.1, ...), custom_call_target="tpu_custom_call" | custom-call | tf_op jit(solution)/shard_map/pallas_call | solution.py:470
  252.3 0.0 copy-start
  252.3 2.4 copy.13
  254.7 0.0 copy-done
  254.7 1.1 copy.14
  (4 shorter events, 0.0 us)
Async XLA Ops:
  252.3 2.4 copy-start

commit v2 on v1

v2 whole, which is shorter than its diff:
```python
import functools

import jax
import jax.numpy as jnp
from jax import lax
from jax.experimental import pallas as pl
from jax.experimental.pallas import tpu as pltpu
from jax.sharding import PartitionSpec as P

MESH = pl.DeviceIdType.MESH
ITERS = 16
RELAX = 0.1
DRAG = 0.5
TURN = 0.3
TILT = 0.05
KEEP = 1.0 / (1.0 + RELAX)

N_GX = 8
N_GY = 16
N_DEV = 128
LEGS = 2
HALO = 2 * ITERS // LEGS
SIDE = 2 * ITERS
ROWS = 128
EXT = ROWS + 2 * HALO
STEP = EXT // 8
TILES_X = 8
CT = TILES_X + 1
UNROLL = 2

MASS, STRENGTH, ZONAL, MERID, SUM, DIFF, SHEAR, SHARE, FORCE_X, FORCE_Y = range(10)
STATIC = 8
FIELDS = 10
FIRST, SECOND, BACK_SLOT, RECV_SLOT, EARLY, LATE = range(6)


def peers():
    order = []
    for n in range(32):
        j = (n * 13) % 32
        dx, dy, dc = j // 8, (j // 2) % 4, j % 2
        off = (n + n // 4 + 3 * dx + dy) % 4 if (dx, dy, dc) != (0, 0, 0) else 0
        order.append((dx, dy, dc, off))
    return order


def each_peer(visit, first=0, last=4):
    gx = lax.axis_index("gx")
    gy = lax.axis_index("gy")
    z, x_lo = gx % 4, gx // 4
    x_hi, y, core = gy // 8, (gy // 2) % 4, gy % 2
    x = x_hi * 2 + x_lo
    xs = [(x + d) % 4 for d in range(4)]
    part_gx = [(v % 2) * 4 for v in xs]
    part_gy = [(v // 2) * 8 for v in xs]
    ys = [((y + d) % 4) * 2 for d in range(4)]
    cores = [core, 1 - core]
    zs = tuple((z + d + first) % 4 for d in range(4))

    def turn(q, zs):
        for dx, dy, dc, off in peers():
            there = (part_gx[dx] + zs[off], part_gy[dx] + ys[dy] + cores[dc])
            if (dx, dy, dc) == (0, 0, 0):
                pl.when(q > 0)(functools.partial(visit, *there))
            else:
                visit(*there)
        return zs[1:] + zs[:1]

    lax.fori_loop(first, last, turn, zs)


def wait_for(ref, sem):
    pltpu.make_async_copy(ref, ref, sem).wait()


def aligned(start, size=8):
    return pl.ds(pl.multiple_of(start, 8), size)


def left_right(row, lane):
    n = len(row)
    left = [pltpu.roll(jnp.where(lane == 127, row[j - 1], row[j]), 1, 1) for j in range(n)]
    right = [pltpu.roll(jnp.where(lane == 0, row[(j + 1) % n], row[j]), 127, 1) for j in range(n)]
    return left, right


def fill_table(route, table, me):
    shape = (N_DEV, N_DEV)
    sub = lax.broadcasted_iota(jnp.int32, shape, 0)
    lane = lax.broadcasted_iota(jnp.int32, shape, 1)
    diagonal = sub == lane

    def to_column(row):
        return jnp.sum(jnp.where(diagonal, row, 0), axis=1, keepdims=True)

    def to_row(column):
        return jnp.sum(jnp.where(diagonal, column, 0), axis=0, keepdims=True)

    mine = jnp.right_shift(route[pl.ds(me, 1), :], 7)
    column = to_column(mine)
    hit = column == lane
    table[pl.ds(FIRST, 1), :] = jnp.min(jnp.where(hit, sub, N_DEV - 1), axis=0, keepdims=True)
    table[pl.ds(SECOND, 1), :] = jnp.max(jnp.where(hit, sub, 0), axis=0, keepdims=True)
    rank = jnp.max(jnp.where((column == mine) & (sub < lane), 1, 0), axis=0, keepdims=True)
    table[pl.ds(BACK_SLOT, 1), :] = mine * 2 + rank
    ids = route[...]
    here = jnp.right_shift(ids, 7) == me
    inside = jnp.bitwise_and(ids, N_DEV - 1)
    first = jnp.min(jnp.where(here, lane, N_DEV), axis=1, keepdims=True)
    second = jnp.max(jnp.where(here, lane, -1), axis=1, keepdims=True)
    early = jnp.sum(jnp.where(lane == first, inside + 1, 0), axis=1, keepdims=True) - 1
    late = jnp.sum(jnp.where(lane == second, inside + 1, 0), axis=1, keepdims=True) - 1
    slot = jnp.where(late == lane, 2 * sub + 1, jnp.where(early == lane, 2 * sub, 0))
    table[pl.ds(RECV_SLOT, 1), :] = jnp.max(slot, axis=0, keepdims=True)
    table[pl.ds(EARLY, 1), :] = to_row(jnp.maximum(early, 0))
    table[pl.ds(LATE, 1), :] = to_row(jnp.maximum(late, 0))
    table[pl.ds(6, 2), :] = jnp.zeros((2, N_DEV), jnp.int32)


def kernel(
    route, ocean, mask, mass, strength, velocity, stress,
    out_velocity, out_stress,
    routes, table, place, oc, outgoing, arrived, ext, ext_mask,
    to_east, to_west, from_west, from_east, force_to_east, force_to_west, force_from_west, force_from_east,
    nat, from_south, from_north, final, tiles, returning, arrived_back,
    cu, cv, cxx, cyy, csh, cstr, ks, km, kfx, kfy, ka, kb,
    in_sem, a2a_sem, halo_sem,
):
    gx = lax.axis_index("gx")
    gy = lax.axis_index("gy")
    me = gx * N_GY + gy
    top = gy == N_GY - 1
    inner = pl.ds(HALO, ROWS)
    lane = lax.broadcasted_iota(jnp.int32, (8, 128), 1)

    pltpu.make_async_copy(route, routes, in_sem.at[3]).start()
    pltpu.make_async_copy(ocean, oc, in_sem.at[0]).start()
    for j in range(TILES_X):
        cols = pl.ds(j * 128, 128)
        pltpu.make_async_copy(mass.at[:, cols], ext.at[MASS, j, inner], in_sem.at[1]).start()
        pltpu.make_async_copy(strength.at[:, cols], ext.at[STRENGTH, j, inner], in_sem.at[1]).start()
        pltpu.make_async_copy(velocity.at[:, :, cols], ext.at[pl.ds(ZONAL, 2), j, inner], in_sem.at[1]).start()
        pltpu.make_async_copy(stress.at[:, :, cols], ext.at[pl.ds(SUM, 3), j, inner], in_sem.at[1]).start()
        pltpu.make_async_copy(mask.at[:, cols], ext_mask.at[j], in_sem.at[2]).start()

    barrier = pltpu.get_barrier_semaphore()

    def greet(a, b):
        pl.semaphore_signal(barrier, inc=1, device_id=(a, b), device_id_type=MESH)

    each_peer(greet)

    wait_for(routes, in_sem.at[3])
    fill_table(routes, table, me)
    to_place = pltpu.make_async_copy(table, place, in_sem.at[4])
    to_place.start()

    wait_for(ext_mask, in_sem.at[2])

    def shares(i, carry):
        for j in range(TILES_X):
            ext[SHARE, j, aligned(HALO + i * 8)] = ext_mask[j, aligned(i * 8)].astype(jnp.float32)
        return carry

    lax.fori_loop(0, ROWS // 8, shares, 0)
    wait_for(ext.at[pl.ds(0, STATIC - 1), pl.ds(0, TILES_X), inner], in_sem.at[1])

    def gather_columns(first, count, east_out, west_out):
        def body(i, carry):
            rows = aligned(HALO + i * 8)
            for g in range((count + 3) // 4):
                e = w = None
                for q in range(min(4, count - 4 * g)):
                    f = first + 4 * g + q
                    a = pltpu.roll(ext[f, TILES_X - 1, rows], (SIDE * (q + 1)) % 128, 1)
                    b = ext[f, 0, rows]
                    if q:
                        b = pltpu.roll(b, SIDE * q, 1)
                    e = a if q == 0 else jnp.where(lane < SIDE * q, e, a)
                    w = b if q == 0 else jnp.where(lane < SIDE * q, w, b)
                east_out[g, aligned(i * 8)] = e
                west_out[g, aligned(i * 8)] = w
            return carry

        lax.fori_loop(0, ROWS // 8, body, 0)

    def spread_columns(first, count, west_in, east_in):
        def body(i, carry):
            rows = aligned(HALO + i * 8)
            for g in range((count + 3) // 4):
                e = east_in[g, aligned(i * 8)]
                w = west_in[g, aligned(i * 8)]
                for q in range(min(4, count - 4 * g)):
                    right = pltpu.roll(e, 128 - SIDE * q, 1) if q else e
                    left = pltpu.roll(w, 128 - SIDE * (q + 1), 1) if q < 3 else w
                    ext[first + 4 * g + q, TILES_X, rows] = jnp.where(lane < 64, right, left)
            return carry

        lax.fori_loop(0, ROWS // 8, body, 0)

    def columns(east_out, west_out, west_in, east_in, sems):
        a = pltpu.make_async_remote_copy(
            east_out, west_in, halo_sem.at[sems], halo_sem.at[sems + 1],
            device_id=((gx + 1) % N_GX, gy), device_id_type=MESH)
        b = pltpu.make_async_remote_copy(
            west_out, east_in, halo_sem.at[sems + 2], halo_sem.at[sems + 3],
            device_id=((gx + N_GX - 1) % N_GX, gy), device_id_type=MESH)
        return a, b

    north_gy = jnp.minimum(gy + 1, N_GY - 1)
    south_gy = jnp.maximum(gy - 1, 0)

    def rows_start(upper, lower, south, north, sems):
        to_north = pltpu.make_async_remote_copy(
            upper, south, halo_sem.at[sems], halo_sem.at[sems + 1],
            device_id=(gx, north_gy), device_id_type=MESH)
        to_partner = pltpu.make_async_remote_copy(
            upper, north, halo_sem.at[sems], halo_sem.at[sems + 3],
            device_id=(N_GX - 1 - gx, gy), device_id_type=MESH)
        to_south = pltpu.make_async_remote_copy(
            lower, north, halo_sem.at[sems + 2], halo_sem.at[sems + 3],
            device_id=(gx, south_gy), device_id_type=MESH)
        pl.when(jnp.logical_not(top))(to_north.start)
        pl.when(top)(to_partner.start)
        pl.when(gy > 0)(to_south.start)

    def rows_wait(upper, lower, south, north, sems):
        wait_for(north, halo_sem.at[sems + 3])
        wait_for(upper, halo_sem.at[sems])

        @pl.when(gy > 0)
        def _():
            wait_for(south, halo_sem.at[sems + 1])
            wait_for(lower, halo_sem.at[sems + 2])

    def strips(first, count):
        return tuple(
            ext.at[pl.ds(first, count), :, pl.ds(at, HALO)] for at in (ROWS, HALO, 0, HALO + ROWS))

    back_sub = 7 - lax.broadcasted_iota(jnp.int32, (8, 128), 0)
    back_lane = 127 - lane

    def turned(x):
        x = jnp.take_along_axis(x, back_lane, axis=1)
        return jnp.take_along_axis(x, back_sub, axis=0)

    def fold(ref, f, base, sign):
        for p in range(HALO // 16):
            here = pl.ds(base + p * 8, 8)
            there = pl.ds(base + HALO - 8 - p * 8, 8)

            def body(j, carry):
                a, b = ref[f, j, here], ref[f, TILES_X - 1 - j, there]
                ref[f, j, here] = turned(b) * sign
                ref[f, TILES_X - 1 - j, there] = turned(a) * sign
                return carry

            lax.fori_loop(0, TILES_X, body, 0)
            a, b = ref[f, TILES_X, here], ref[f, TILES_X, there]
            ref[f, TILES_X, here] = turned(b) * sign
            ref[f, TILES_X, there] = turned(a) * sign

    static_cols = columns(to_east, to_west, from_west, from_east, 0)
    force_cols = columns(force_to_east, force_to_west, force_from_west, force_from_east, 4)
    static_rows = strips(0, STATIC)
    force_rows = strips(FORCE_X, 2)

    gather_columns(0, STATIC, to_east, to_west)

    to_place.wait()
    wait_for(oc, in_sem.at[0])

    def pack(i, carry):
        for h in range(4):
            outgoing[i * 8 + 2 * h] = oc[place[FIRST, i * 4 + h]]
            outgoing[i * 8 + 2 * h + 1] = oc[place[SECOND, i * 4 + h]]
        return carry

    lax.fori_loop(0, N_DEV // 4, pack, 0)
    pl.semaphore_wait(barrier, N_DEV - 1)

    def send_forcing(a, b):
        pltpu.make_async_remote_copy(
            outgoing.at[pl.ds((a * N_GY + b) * 2, 2)], arrived.at[pl.ds(me * 2, 2)],
            a2a_sem.at[0], a2a_sem.at[1], device_id=(a, b), device_id_type=MESH,
        ).start()

    for copy in static_cols:
        copy.start()
    each_peer(send_forcing, 0, 1)
    for copy in static_cols:
        copy.wait()
    spread_columns(0, STATIC, from_west, from_east)
    rows_start(*static_rows, 8)
    each_peer(send_forcing, 1, 4)
    for h in range(2):
        arrived[me * 2 + h] = outgoing[me * 2 + h]

    @pl.when(gy == 0)
    def _():
        zero = jnp.zeros((8, 128), jnp.float32)

        def clear(j, carry):
            for p in range(HALO // 8):
                for f in range(FIELDS):
                    ext[f, j, pl.ds(p * 8, 8)] = zero + 1.0 if f == MASS else zero
            return carry

        lax.fori_loop(0, CT, clear, 0)

    rows_wait(*static_rows, 8)

    @pl.when(top)
    def _():
        for f in range(STATIC):
            fold(ext, f, HALO + ROWS, -1.0 if f in (ZONAL, MERID) else 1.0)

    def arrange(r, carry):
        rows = pl.ds(r, 8, stride=STEP)
        for j in range(CT):
            share = ext[SHARE, j, rows]
            m = ext[MASS, j, rows]
            strong = ext[STRENGTH, j, rows]
            a = m + DRAG
            b = TURN * m
            scale = share / (a * a + b * b)
            km[r, j] = m
            ka[r, j] = a * scale
            kb[r, j] = b * scale
            ks[r, j] = (0.0125 * KEEP) * strong
            cstr[r + 1, j] = strong
            cu[r + 1, j] = ext[ZONAL, j, rows] * share
            cv[r + 1, j] = ext[MERID, j, rows] * share
            both = 0.25 * (ext[SUM, j, rows] + strong)
            apart = 0.25 * ext[DIFF, j, rows]
            cxx[r + 1, j] = both + apart
            cyy[r + 1, j] = both - apart
            csh[r + 1, j] = 0.5 * ext[SHEAR, j, rows]
        return carry

    lax.fori_loop(0, STEP, arrange, 0)

    def ghosts(*refs):
        for ref in refs:
            for j in range(CT):
                ref[0, j] = pltpu.roll(ref[STEP, j], 1, 0)
                ref[STEP + 1, j] = pltpu.roll(ref[1, j], 7, 0)

    ghosts(cu, cv, cstr)

    wait_for(arrived.at[pl.ds(0, 2 * N_DEV - 2)], a2a_sem.at[1])
    wait_for(outgoing.at[pl.ds(0, 2 * N_DEV - 2)], a2a_sem.at[0])

    def forces(i, carry):
        rows = aligned(HALO + i * 8)
        for j in range(TILES_X):
            tile = arrived[place[RECV_SLOT, i * TILES_X + j]]
            m = TILT * ext[MASS, j, rows]
            ext[FORCE_X, j, rows] = tile[0] + m * tile[2]
            ext[FORCE_Y, j, rows] = tile[1] + m * tile[3]
        return carry

    lax.fori_loop(0, ROWS // 8, forces, 0)
    gather_columns(FORCE_X, 2, force_to_east, force_to_west)
    for copy in force_cols:
        copy.start()
    for copy in force_cols:
        copy.wait()
    spread_columns(FORCE_X, 2, force_from_west, force_from_east)
    rows_start(*force_rows, 12)
    rows_wait(*force_rows, 12)

    @pl.when(top)
    def _():
        fold(ext, FORCE_X, HALO + ROWS, -1.0)
        fold(ext, FORCE_Y, HALO + ROWS, -1.0)

    def arrange_forces(r, carry):
        rows = pl.ds(r, 8, stride=STEP)
        left, right = left_right([cstr[r + 1, j] for j in range(CT)], lane)
        for j in range(CT):
            kfx[r, j] = ext[FORCE_X, j, rows] - 0.25 * (right[j] - left[j])
            kfy[r, j] = ext[FORCE_Y, j, rows] - 0.25 * (cstr[r + 2, j] - cstr[r, j])
        return carry

    lax.fori_loop(0, STEP, arrange_forces, 0)

    def stresses(i, carry):
        for r in [i * UNROLL + h for h in range(UNROLL)]:
            u_left, u_right = left_right([cu[r + 1, j] for j in range(CT)], lane)
            v_left, v_right = left_right([cv[r + 1, j] for j in range(CT)], lane)
            for j in range(CT):
                ux = u_right[j] - u_left[j]
                vx = v_right[j] - v_left[j]
                uy = cu[r + 2, j] - cu[r, j]
                vy = cv[r + 2, j] - cv[r, j]
                div = ux + vy
                ten = ux - vy
                shr = uy + vx
                div2 = div + div
                w = ks[r, j] * lax.rsqrt(div2 * div2 + ten * ten + shr * shr + 16.0)
                div4 = div2 + div2
                cxx[r + 1, j] = KEEP * cxx[r + 1, j] + w * (div4 + ten)
                cyy[r + 1, j] = KEEP * cyy[r + 1, j] + w * (div4 - ten)
                csh[r + 1, j] = KEEP * csh[r + 1, j] + w * shr
        return carry

    def momentum(i, carry):
        for r in [i * UNROLL + h for h in range(UNROLL)]:
            xx_left, xx_right = left_right([cxx[r + 1, j] for j in range(CT)], lane)
            sh_left, sh_right = left_right([csh[r + 1, j] for j in range(CT)], lane)
            for j in range(CT):
                px = (xx_right[j] - xx_left[j]) + (csh[r + 2, j] - csh[r, j])
                py = (sh_right[j] - sh_left[j]) + (cyy[r + 2, j] - cyy[r, j])
                m = km[r, j]
                rx = m * cu[r + 1, j] + (px + kfx[r, j])
                ry = m * cv[r + 1, j] + (py + kfy[r, j])
                a = ka[r, j]
                b = kb[r, j]
                cu[r + 1, j] = a * rx + b * ry
                cv[r + 1, j] = a * ry - b * rx
        return carry

    def subcycle(t, carry):
        lax.fori_loop(0, STEP // UNROLL, stresses, 0)
        ghosts(cyy, csh)
        lax.fori_loop(0, STEP // UNROLL, momentum, 0)
        ghosts(cu, cv)
        return carry

    carried = (cu, cv, cxx, cyy, csh)

    def to_grid_order(r, carry):
        for f, ref in enumerate(carried):
            for j in range(CT):
                nat[f, j, pl.ds(r, 8, stride=STEP)] = ref[r + 1, j]
        return carry

    def from_grid_order(r, carry):
        for f, ref in enumerate(carried):
            for j in range(CT):
                ref[r + 1, j] = nat[f, j, pl.ds(r, 8, stride=STEP)]
        return carry

    lax.fori_loop(0, ITERS // LEGS, subcycle, 0)
    lax.fori_loop(0, STEP, to_grid_order, 0)
    state_rows = (nat.at[:, :, pl.ds(ROWS, HALO)], nat.at[:, :, pl.ds(HALO, HALO)], from_south, from_north)
    rows_start(*state_rows, 16)
    rows_wait(*state_rows, 16)

    @pl.when(top)
    def _():
        for f in range(5):
            fold(from_north, f, 0, -1.0 if f < 2 else 1.0)

    def take_rows(j, carry):
        for f in range(5):
            for p in range(HALO // 8):
                nat[f, j, pl.ds(HALO + ROWS + p * 8, 8)] = from_north[f, j, pl.ds(p * 8, 8)]
        return carry

    def take_south_rows(j, carry):
        for f in range(5):
            for p in range(HALO // 8):
                nat[f, j, pl.ds(p * 8, 8)] = from_south[f, j, pl.ds(p * 8, 8)]
        return carry

    lax.fori_loop(0, CT, take_rows, 0)

    @pl.when(gy > 0)
    def _():
        lax.fori_loop(0, CT, take_south_rows, 0)

    lax.fori_loop(0, STEP, from_grid_order, 0)
    ghosts(cu, cv)
    lax.fori_loop(0, ITERS // LEGS, subcycle, 0)
    lax.fori_loop(0, STEP, to_grid_order, 0)

    def to_tiles(i, carry):
        rows = aligned(HALO + i * 8)
        for j in range(TILES_X):
            tiles[i * TILES_X + j, 0] = nat[0, j, rows]
            tiles[i * TILES_X + j, 1] = nat[1, j, rows]
        return carry

    lax.fori_loop(0, ROWS // 8, to_tiles, 0)

    def pack_back(i, carry):
        for h in range(4):
            returning[i * 8 + 2 * h] = tiles[place[EARLY, i * 4 + h]]
            returning[i * 8 + 2 * h + 1] = tiles[place[LATE, i * 4 + h]]
        return carry

    lax.fori_loop(0, N_DEV // 4, pack_back, 0)

    def send_back(a, b):
        pltpu.make_async_remote_copy(
            returning.at[pl.ds((a * N_GY + b) * 2, 2)], arrived_back.at[pl.ds(me * 2, 2)],
            a2a_sem.at[2], a2a_sem.at[3], device_id=(a, b), device_id_type=MESH,
        ).start()

    each_peer(send_back)
    for h in range(2):
        arrived_back[me * 2 + h] = returning[me * 2 + h]

    def finish(i, carry):
        rows = aligned(HALO + i * 8)
        for j in range(TILES_X):
            xx = nat[2, j, rows]
            yy = nat[3, j, rows]
            final[0, j, aligned(i * 8)] = 2.0 * (xx + yy) - ext[STRENGTH, j, rows]
            final[1, j, aligned(i * 8)] = 2.0 * (xx - yy)
            final[2, j, aligned(i * 8)] = 2.0 * nat[4, j, rows]
        return carry

    lax.fori_loop(0, ROWS // 8, finish, 0)
    for j in range(TILES_X):
        pltpu.make_async_copy(final.at[:, j], out_stress.at[:, :, pl.ds(j * 128, 128)], in_sem.at[1]).start()

    wait_for(arrived_back.at[pl.ds(0, 2 * N_DEV - 2)], a2a_sem.at[3])
    wait_for(returning.at[pl.ds(0, 2 * N_DEV - 2)], a2a_sem.at[2])

    def unpack(i, carry):
        for h in range(8):
            out_velocity[i * 8 + h] = arrived_back[place[BACK_SLOT, i * 8 + h]]
        return carry

    lax.fori_loop(0, N_DEV // 8, unpack, 0)
    wait_for(final, in_sem.at[1])


def local(ocean_forcing, route, land_mask, mass, strength, velocity_start, stress_start):
    f32, i32 = jnp.float32, jnp.int32
    hbm = pl.BlockSpec(memory_space=pl.ANY)
    ghosted = pltpu.VMEM((STEP + 2, CT, 8, 128), f32)
    plain = pltpu.VMEM((STEP, CT, 8, 128), f32)
    side = pltpu.VMEM((STATIC // 4, ROWS, 128), f32)
    force_side = pltpu.VMEM((1, ROWS, 128), f32)
    strip = pltpu.VMEM((5, CT, HALO, 128), f32)
    return pl.pallas_call(
        kernel,
        out_shape=(
            jax.ShapeDtypeStruct((N_DEV, 2, 8, 128), f32),
            jax.ShapeDtypeStruct((3, ROWS, TILES_X * 128), f32),
        ),
        in_specs=[hbm] * 7,
        out_specs=(pl.BlockSpec(memory_space=pltpu.VMEM), hbm),
        scratch_shapes=[
            pltpu.VMEM((N_DEV, N_DEV), i32),
            pltpu.VMEM((8, N_DEV), i32),
            pltpu.SMEM((8, N_DEV), i32),
            pltpu.VMEM((N_DEV, 4, 8, 128), f32),
            pltpu.VMEM((2 * N_DEV, 4, 8, 128), f32),
            pltpu.VMEM((2 * N_DEV, 4, 8, 128), f32),
            pltpu.VMEM((FIELDS, CT, EXT, 128), f32),
            pltpu.VMEM((TILES_X, ROWS, 128), i32),
            side, side, side, side,
            force_side, force_side, force_side, force_side,
            pltpu.VMEM((5, CT, EXT, 128), f32),
            strip, strip,
            pltpu.VMEM((3, TILES_X, ROWS, 128), f32),
            pltpu.VMEM((N_DEV, 2, 8, 128), f32),
            pltpu.VMEM((2 * N_DEV, 2, 8, 128), f32),
            pltpu.VMEM((2 * N_DEV, 2, 8, 128), f32),
            ghosted, ghosted, ghosted, ghosted, ghosted, ghosted,
            plain, plain, plain, plain, plain, plain,
            pltpu.SemaphoreType.DMA((5,)),
            pltpu.SemaphoreType.DMA((4,)),
            pltpu.SemaphoreType.DMA((20,)),
        ],
        compiler_params=pltpu.CompilerParams(
            collective_id=0, has_side_effects=True, vmem_limit_bytes=56 * 1024 * 1024),
    )(route.reshape(N_DEV, N_DEV), ocean_forcing, land_mask, mass, strength, velocity_start, stress_start)


def solution(mesh):
    placed = (
        P(("gx", "gy"), None, None, None),
        P(),
        P("gy", "gx"),
        P("gy", "gx"),
        P("gy", "gx"),
        P(None, "gy", "gx"),
        P(None, "gy", "gx"),
    )
    return jax.shard_map(
        local,
        mesh=mesh,
        in_specs=placed,
        out_specs=(P(("gx", "gy"), None, None, None), P(None, "gy", "gx")),
        check_vma=False,
    )
```

time: 256 us -> 185 us (0.72)
  Pallas kernels: 245 us -> 181 us
  other arithmetic: 4.89 us -> 0 us
    pallas_call x1, Pallas kernels: 245 us -> 181 us  [local(): pl.pallas_call(kernel, out_shape=(jax.ShapeDtypeStruct((N_DEV, 2, 8, 128)...]
where the time goes in v2:
time: 185 us
  Pallas kernels  181 us (98%)
  local copies, waits for them, and re-layouts  3.53 us (2%)
    pallas_call x1, Pallas kernels, local(): pl.pallas_call(kernel, out_shape=(jax.ShapeDtypeStruct((N_DEV, 2, 8, 128)...  181 us

profile of v2, /device:TPU:1, one launch (start us, length us, event | category | flops | bytes accessed | tf_op | source)
XLA Modules:
  0.0 184.9 jit_solution(16940882424294863729)
XLA Ops:
  0.6 180.7 %shard_map.86 = (f32[128,2,8,128]{3,2,1,0:T(8,128)}, f32[3,128,1024]{2,1,0:T(8,128)}) custom-call(s32[128,128]{1,0:T(8,128)} %bitcast.1, f32[128,4,8,128]{3,2,1,0:T(8,128)} %ocean.1, s32[128,1024]{1,0:T(8,128)} %mask.1, f32[128,1024]{1,0:T(8,128)} %mass.1, f32[128,1024]{1,0:T(8,128)} %strength.1, f32[2,128,1024]{2,1,0:T(8,128)} %velocity.1, ...), custom_call_target="tpu_custom_call" | custom-call | tf_op jit(solution)/shard_map/pallas_call | solution.py:540
  181.4 0.0 copy-start
  181.4 2.4 %copy.11 = f32[128,2,8,128]{3,2,1,0:T(8,128)} copy(f32[128,2,8,128]{3,2,1,0:T(8,128)} %get-tuple-element.4) | data formatting | bytes 2097152
  183.7 0.0 copy-done
  183.7 1.1 copy.12
Async XLA Ops:
  181.4 2.4 %copy-start = (f32[3,128,1024]{2,1,0:T(8,128)S(1)}, f32[3,128,1024]{2,1,0:T(8,128)}, u32[]{:S(2)}) copy-start(f32[3,128,1024]{2,1,0:T(8,128)} %get-tuple-element.5) | copy-start | bytes 4718596

commit v3 on v2

--- a/solution.py
+++ b/solution.py
@@ -26,7 +26,7 @@
 STEP = EXT // 8
 TILES_X = 8
 CT = TILES_X + 1
-UNROLL = 2
+UNROLL = 10
 
 MASS, STRENGTH, ZONAL, MERID, SUM, DIFF, SHEAR, SHARE, FORCE_X, FORCE_Y = range(10)
 STATIC = 8
@@ -385,13 +385,22 @@
 
     lax.fori_loop(0, STEP, arrange_forces, 0)
 
+    def shifted(ref, r):
+        def left(j):
+            return pltpu.roll(jnp.where(lane == 127, ref[r, (j - 1) % CT], ref[r, j]), 1, 1)
+
+        def right(j):
+            return pltpu.roll(jnp.where(lane == 0, ref[r, (j + 1) % CT], ref[r, j]), 127, 1)
+
+        return left, right
+
     def stresses(i, carry):
         for r in [i * UNROLL + h for h in range(UNROLL)]:
-            u_left, u_right = left_right([cu[r + 1, j] for j in range(CT)], lane)
-            v_left, v_right = left_right([cv[r + 1, j] for j in range(CT)], lane)
+            u_left, u_right = shifted(cu, r + 1)
+            v_left, v_right = shifted(cv, r + 1)
             for j in range(CT):
-                ux = u_right[j] - u_left[j]
-                vx = v_right[j] - v_left[j]
+                ux = u_right(j) - u_left(j)
+                vx = v_right(j) - v_left(j)
                 uy = cu[r + 2, j] - cu[r, j]
                 vy = cv[r + 2, j] - cv[r, j]
                 div = ux + vy
@@ -407,11 +416,11 @@
 
     def momentum(i, carry):
         for r in [i * UNROLL + h for h in range(UNROLL)]:
-            xx_left, xx_right = left_right([cxx[r + 1, j] for j in range(CT)], lane)
-            sh_left, sh_right = left_right([csh[r + 1, j] for j in range(CT)], lane)
+            xx_left, xx_right = shifted(cxx, r + 1)
+            sh_left, sh_right = shifted(csh, r + 1)
             for j in range(CT):
-                px = (xx_right[j] - xx_left[j]) + (csh[r + 2, j] - csh[r, j])
-                py = (sh_right[j] - sh_left[j]) + (cyy[r + 2, j] - cyy[r, j])
+                px = (xx_right(j) - xx_left(j)) + (csh[r + 2, j] - csh[r, j])
+                py = (sh_right(j) - sh_left(j)) + (cyy[r + 2, j] - cyy[r, j])
                 m = km[r, j]
                 rx = m * cu[r + 1, j] + (px + kfx[r, j])
                 ry = m * cv[r + 1, j] + (py + kfy[r, j])
@@ -421,59 +430,59 @@
                 cv[r + 1, j] = a * ry - b * rx
         return carry
 
+    carried = (cu, cv, cxx, cyy, csh)
+
+    def to_grid_order(r, carry):
+        for f, ref in enumerate(carried):
+            for j in range(CT):
+                nat[f, j, pl.ds(r, 8, stride=STEP)] = ref[r + 1, j]
+        return carry
+
+    def from_grid_order(r, carry):
+        for f, ref in enumerate(carried):
+            for j in range(CT):
+                ref[r + 1, j] = nat[f, j, pl.ds(r, 8, stride=STEP)]
+        return carry
+
+    state_rows = (nat.at[:, :, pl.ds(ROWS, HALO)], nat.at[:, :, pl.ds(HALO, HALO)], from_south, from_north)
+
+    def take(strip, base):
+        def body(j, carry):
+            for f in range(5):
+                for p in range(HALO // 8):
+                    nat[f, j, pl.ds(base + p * 8, 8)] = strip[f, j, pl.ds(p * 8, 8)]
+            return carry
+
+        lax.fori_loop(0, CT, body, 0)
+
+    def exchange_rows():
+        lax.fori_loop(0, STEP, to_grid_order, 0)
+        rows_start(*state_rows, 16)
+        rows_wait(*state_rows, 16)
+
+        @pl.when(top)
+        def _():
+            for f in range(5):
+                fold(from_north, f, 0, -1.0 if f < 2 else 1.0)
+
+        take(from_north, HALO + ROWS)
+
+        @pl.when(gy > 0)
+        def _():
+            take(from_south, 0)
+
+        lax.fori_loop(0, STEP, from_grid_order, 0)
+        ghosts(cu, cv)
+
     def subcycle(t, carry):
+        pl.when(t == ITERS // LEGS)(exchange_rows)
         lax.fori_loop(0, STEP // UNROLL, stresses, 0)
         ghosts(cyy, csh)
         lax.fori_loop(0, STEP // UNROLL, momentum, 0)
         ghosts(cu, cv)
         return carry
 
-    carried = (cu, cv, cxx, cyy, csh)
-
-    def to_grid_order(r, carry):
-        for f, ref in enumerate(carried):
-            for j in range(CT):
-                nat[f, j, pl.ds(r, 8, stride=STEP)] = ref[r + 1, j]
-        return carry
-
-    def from_grid_order(r, carry):
-        for f, ref in enumerate(carried):
-            for j in range(CT):
-                ref[r + 1, j] = nat[f, j, pl.ds(r, 8, stride=STEP)]
-        return carry
-
-    lax.fori_loop(0, ITERS // LEGS, subcycle, 0)
-    lax.fori_loop(0, STEP, to_grid_order, 0)
-    state_rows = (nat.at[:, :, pl.ds(ROWS, HALO)], nat.at[:, :, pl.ds(HALO, HALO)], from_south, from_north)
-    rows_start(*state_rows, 16)
-    rows_wait(*state_rows, 16)
-
-    @pl.when(top)
-    def _():
-        for f in range(5):
-            fold(from_north, f, 0, -1.0 if f < 2 else 1.0)
-
-    def take_rows(j, carry):
-        for f in range(5):
-            for p in range(HALO // 8):
-                nat[f, j, pl.ds(HALO + ROWS + p * 8, 8)] = from_north[f, j, pl.ds(p * 8, 8)]
-        return carry
-
-    def take_south_rows(j, carry):
-        for f in range(5):
-            for p in range(HALO // 8):
-                nat[f, j, pl.ds(p * 8, 8)] = from_south[f, j, pl.ds(p * 8, 8)]
-        return carry
-
-    lax.fori_loop(0, CT, take_rows, 0)
-
-    @pl.when(gy > 0)
-    def _():
-        lax.fori_loop(0, CT, take_south_rows, 0)
-
-    lax.fori_loop(0, STEP, from_grid_order, 0)
-    ghosts(cu, cv)
-    lax.fori_loop(0, ITERS // LEGS, subcycle, 0)
+    lax.fori_loop(0, ITERS, subcycle, 0)
     lax.fori_loop(0, STEP, to_grid_order, 0)
 
     def to_tiles(i, carry):

time: 185 us -> 164 us (0.89)
  Pallas kernels: 181 us -> 160 us
    pallas_call x1, Pallas kernels: 181 us -> 160 us  [local(): pl.pallas_call(kernel, out_shape=(jax.ShapeDtypeStruct((N_DEV, 2, 8, 128)...]
where the time goes in v3:
time: 164 us
  Pallas kernels  160 us (98%)
  local copies, waits for them, and re-layouts  3.53 us (2%)
    pallas_call x1, Pallas kernels, local(): pl.pallas_call(kernel, out_shape=(jax.ShapeDtypeStruct((N_DEV, 2, 8, 128)...  160 us
    unnamed x4, local copies, waits for them, and re-layouts  3.53 us

profile of v3, /device:TPU:1, one launch (start us, length us, event | category | flops | bytes accessed | tf_op | source)
XLA Modules:
  0.0 163.8 jit_solution(12249039975333122620)
XLA Ops:
  0.6 159.6 %shard_map.86 = (f32[128,2,8,128]{3,2,1,0:T(8,128)}, f32[3,128,1024]{2,1,0:T(8,128)}) custom-call(s32[128,128]{1,0:T(8,128)} %bitcast.1, f32[128,4,8,128]{3,2,1,0:T(8,128)} %ocean.1, s32[128,1024]{1,0:T(8,128)} %mask.1, f32[128,1024]{1,0:T(8,128)} %mass.1, f32[128,1024]{1,0:T(8,128)} %strength.1, f32[2,128,1024]{2,1,0:T(8,128)} %velocity.1, ...), custom_call_target="tpu_custom_call" | custom-call | tf_op jit(solution)/shard_map/pallas_call | solution.py:549
  160.2 0.0 copy-start
  160.2 2.4 %copy.11 = f32[128,2,8,128]{3,2,1,0:T(8,128)} copy(f32[128,2,8,128]{3,2,1,0:T(8,128)} %get-tuple-element.4) | data formatting | bytes 2097152
  162.6 0.0 copy-done
  162.6 1.1 copy.12
Async XLA Ops:
  160.2 2.4 %copy-start = (f32[3,128,1024]{2,1,0:T(8,128)S(1)}, f32[3,128,1024]{2,1,0:T(8,128)}, u32[]{:S(2)}) copy-start(f32[3,128,1024]{2,1,0:T(8,128)} %get-tuple-element.5) | copy-start | bytes 4718596

commit v4 on v3

--- a/solution.py
+++ b/solution.py
@@ -120,7 +120,7 @@
 def kernel(
     route, ocean, mask, mass, strength, velocity, stress,
     out_velocity, out_stress,
-    routes, table, place, oc, outgoing, arrived, ext, ext_mask,
+    routes, table, place, oc, mass_tiles, mass_out, mass_in, outgoing, arrived, ext, ext_mask,
     to_east, to_west, from_west, from_east, force_to_east, force_to_west, force_from_west, force_from_east,
     nat, from_south, from_north, final, tiles, returning, arrived_back,
     cu, cv, cxx, cyy, csh, cstr, ks, km, kfx, kfy, ka, kb,
@@ -134,15 +134,16 @@
     lane = lax.broadcasted_iota(jnp.int32, (8, 128), 1)
 
     pltpu.make_async_copy(route, routes, in_sem.at[3]).start()
-    pltpu.make_async_copy(ocean, oc, in_sem.at[0]).start()
+    for j in range(TILES_X):
+        pltpu.make_async_copy(mass.at[:, pl.ds(j * 128, 128)], ext.at[MASS, j, inner], in_sem.at[5]).start()
     for j in range(TILES_X):
         cols = pl.ds(j * 128, 128)
-        pltpu.make_async_copy(mass.at[:, cols], ext.at[MASS, j, inner], in_sem.at[1]).start()
         pltpu.make_async_copy(strength.at[:, cols], ext.at[STRENGTH, j, inner], in_sem.at[1]).start()
         pltpu.make_async_copy(velocity.at[:, :, cols], ext.at[pl.ds(ZONAL, 2), j, inner], in_sem.at[1]).start()
         pltpu.make_async_copy(stress.at[:, :, cols], ext.at[pl.ds(SUM, 3), j, inner], in_sem.at[1]).start()
         pltpu.make_async_copy(mask.at[:, cols], ext_mask.at[j], in_sem.at[2]).start()
 
+    pltpu.make_async_copy(ocean, oc, in_sem.at[0]).start()
     barrier = pltpu.get_barrier_semaphore()
 
     def greet(a, b):
@@ -155,6 +156,24 @@
     to_place = pltpu.make_async_copy(table, place, in_sem.at[4])
     to_place.start()
 
+    wait_for(ext.at[MASS, pl.ds(0, TILES_X), inner], in_sem.at[5])
+
+    def to_mass_tiles(i, carry):
+        for j in range(TILES_X):
+            mass_tiles[i * TILES_X + j] = ext[MASS, j, aligned(HALO + i * 8)]
+        return carry
+
+    lax.fori_loop(0, ROWS // 8, to_mass_tiles, 0)
+    to_place.wait()
+
+    def pack_mass(i, carry):
+        for h in range(8):
+            mass_out[i * 16 + 2 * h] = mass_tiles[place[EARLY, i * 8 + h]]
+            mass_out[i * 16 + 2 * h + 1] = mass_tiles[place[LATE, i * 8 + h]]
+        return carry
+
+    lax.fori_loop(0, N_DEV // 8, pack_mass, 0)
+
     wait_for(ext_mask, in_sem.at[2])
 
     def shares(i, carry):
@@ -163,7 +182,7 @@
         return carry
 
     lax.fori_loop(0, ROWS // 8, shares, 0)
-    wait_for(ext.at[pl.ds(0, STATIC - 1), pl.ds(0, TILES_X), inner], in_sem.at[1])
+    wait_for(ext.at[pl.ds(STRENGTH, STATIC - 2), pl.ds(0, TILES_X), inner], in_sem.at[1])
 
     def gather_columns(first, count, east_out, west_out):
         def body(i, carry):
@@ -244,21 +263,20 @@
         x = jnp.take_along_axis(x, back_lane, axis=1)
         return jnp.take_along_axis(x, back_sub, axis=0)
 
-    def fold(ref, f, base, sign):
-        for p in range(HALO // 16):
-            here = pl.ds(base + p * 8, 8)
-            there = pl.ds(base + HALO - 8 - p * 8, 8)
-
-            def body(j, carry):
-                a, b = ref[f, j, here], ref[f, TILES_X - 1 - j, there]
-                ref[f, j, here] = turned(b) * sign
-                ref[f, TILES_X - 1 - j, there] = turned(a) * sign
-                return carry
-
-            lax.fori_loop(0, TILES_X, body, 0)
-            a, b = ref[f, TILES_X, here], ref[f, TILES_X, there]
-            ref[f, TILES_X, here] = turned(b) * sign
-            ref[f, TILES_X, there] = turned(a) * sign
+    def fold(ref, first, count, base, odd):
+        tall = HALO // 8
+
+        def body(f, carry):
+            sign = jnp.where((f >= odd[0]) & (f < odd[1]), -1.0, 1.0)
+            for j in range(TILES_X // 2 + 1):
+                pair = (j, TILES_X - 1 - j) if j < TILES_X // 2 else (TILES_X,)
+                old = [[ref[f, c, pl.ds(base + p * 8, 8)] for c in pair] for p in range(tall)]
+                for p in range(tall):
+                    for n, c in enumerate(pair):
+                        ref[f, c, pl.ds(base + p * 8, 8)] = turned(old[tall - 1 - p][len(pair) - 1 - n]) * sign
+            return carry
+
+        lax.fori_loop(first, first + count, body, 0)
 
     static_cols = columns(to_east, to_west, from_west, from_east, 0)
     force_cols = columns(force_to_east, force_to_west, force_from_west, force_from_east, 4)
@@ -267,34 +285,46 @@
 
     gather_columns(0, STATIC, to_east, to_west)
 
-    to_place.wait()
-    wait_for(oc, in_sem.at[0])
-
-    def pack(i, carry):
-        for h in range(4):
-            outgoing[i * 8 + 2 * h] = oc[place[FIRST, i * 4 + h]]
-            outgoing[i * 8 + 2 * h + 1] = oc[place[SECOND, i * 4 + h]]
-        return carry
-
-    lax.fori_loop(0, N_DEV // 4, pack, 0)
     pl.semaphore_wait(barrier, N_DEV - 1)
 
-    def send_forcing(a, b):
+    def send_mass(a, b):
         pltpu.make_async_remote_copy(
-            outgoing.at[pl.ds((a * N_GY + b) * 2, 2)], arrived.at[pl.ds(me * 2, 2)],
+            mass_out.at[pl.ds((a * N_GY + b) * 2, 2)], mass_in.at[pl.ds(me * 2, 2)],
+            a2a_sem.at[4], a2a_sem.at[5], device_id=(a, b), device_id_type=MESH,
+        ).start()
+
+    def pack_forces(d):
+        for h in range(2):
+            tile = oc[place[FIRST + h, d]]
+            m = TILT * mass_in[d * 2 + h]
+            outgoing[d * 2 + h, 0] = tile[0] + m * tile[2]
+            outgoing[d * 2 + h, 1] = tile[1] + m * tile[3]
+
+    def send_forces(a, b):
+        d = a * N_GY + b
+        pack_forces(d)
+        pltpu.make_async_remote_copy(
+            outgoing.at[pl.ds(d * 2, 2)], arrived.at[pl.ds(me * 2, 2)],
             a2a_sem.at[0], a2a_sem.at[1], device_id=(a, b), device_id_type=MESH,
         ).start()
 
     for copy in static_cols:
         copy.start()
-    each_peer(send_forcing, 0, 1)
+    each_peer(send_mass)
+    for h in range(2):
+        mass_in[me * 2 + h] = mass_out[me * 2 + h]
     for copy in static_cols:
         copy.wait()
     spread_columns(0, STATIC, from_west, from_east)
     rows_start(*static_rows, 8)
-    each_peer(send_forcing, 1, 4)
+
+    wait_for(oc, in_sem.at[0])
+    wait_for(mass_in.at[pl.ds(0, 2 * N_DEV - 2)], a2a_sem.at[5])
+    each_peer(send_forces)
+    pack_forces(me)
     for h in range(2):
         arrived[me * 2 + h] = outgoing[me * 2 + h]
+    wait_for(mass_out.at[pl.ds(0, 2 * N_DEV - 2)], a2a_sem.at[4])
 
     @pl.when(gy == 0)
     def _():
@@ -312,8 +342,7 @@
 
     @pl.when(top)
     def _():
-        for f in range(STATIC):
-            fold(ext, f, HALO + ROWS, -1.0 if f in (ZONAL, MERID) else 1.0)
+        fold(ext, 0, STATIC, HALO + ROWS, (ZONAL, MERID + 1))
 
     def arrange(r, carry):
         rows = pl.ds(r, 8, stride=STEP)
@@ -355,9 +384,8 @@
         rows = aligned(HALO + i * 8)
         for j in range(TILES_X):
             tile = arrived[place[RECV_SLOT, i * TILES_X + j]]
-            m = TILT * ext[MASS, j, rows]
-            ext[FORCE_X, j, rows] = tile[0] + m * tile[2]
-            ext[FORCE_Y, j, rows] = tile[1] + m * tile[3]
+            ext[FORCE_X, j, rows] = tile[0]
+            ext[FORCE_Y, j, rows] = tile[1]
         return carry
 
     lax.fori_loop(0, ROWS // 8, forces, 0)
@@ -372,8 +400,7 @@
 
     @pl.when(top)
     def _():
-        fold(ext, FORCE_X, HALO + ROWS, -1.0)
-        fold(ext, FORCE_Y, HALO + ROWS, -1.0)
+        fold(ext, FORCE_X, 2, HALO + ROWS, (FORCE_X, FORCE_Y + 1))
 
     def arrange_forces(r, carry):
         rows = pl.ds(r, 8, stride=STEP)
@@ -432,11 +459,14 @@
 
     carried = (cu, cv, cxx, cyy, csh)
 
-    def to_grid_order(r, carry):
-        for f, ref in enumerate(carried):
-            for j in range(CT):
-                nat[f, j, pl.ds(r, 8, stride=STEP)] = ref[r + 1, j]
-        return carry
+    def to_grid_order(first, count):
+        def body(r, carry):
+            for f in range(first, first + count):
+                for j in range(CT):
+                    nat[f, j, pl.ds(r, 8, stride=STEP)] = carried[f][r + 1, j]
+            return carry
+
+        lax.fori_loop(0, STEP, body, 0)
 
     def from_grid_order(r, carry):
         for f, ref in enumerate(carried):
@@ -456,14 +486,13 @@
         lax.fori_loop(0, CT, body, 0)
 
     def exchange_rows():
-        lax.fori_loop(0, STEP, to_grid_order, 0)
+        to_grid_order(0, 5)
         rows_start(*state_rows, 16)
         rows_wait(*state_rows, 16)
 
         @pl.when(top)
         def _():
-            for f in range(5):
-                fold(from_north, f, 0, -1.0 if f < 2 else 1.0)
+            fold(from_north, 0, 5, 0, (0, 2))
 
         take(from_north, HALO + ROWS)
 
@@ -483,7 +512,7 @@
         return carry
 
     lax.fori_loop(0, ITERS, subcycle, 0)
-    lax.fori_loop(0, STEP, to_grid_order, 0)
+    to_grid_order(0, 2)
 
     def to_tiles(i, carry):
         rows = aligned(HALO + i * 8)
@@ -494,23 +523,23 @@
 
     lax.fori_loop(0, ROWS // 8, to_tiles, 0)
 
-    def pack_back(i, carry):
-        for h in range(4):
-            returning[i * 8 + 2 * h] = tiles[place[EARLY, i * 4 + h]]
-            returning[i * 8 + 2 * h + 1] = tiles[place[LATE, i * 4 + h]]
-        return carry
-
-    lax.fori_loop(0, N_DEV // 4, pack_back, 0)
+    def pack_back(d):
+        returning[d * 2] = tiles[place[EARLY, d]]
+        returning[d * 2 + 1] = tiles[place[LATE, d]]
 
     def send_back(a, b):
+        d = a * N_GY + b
+        pack_back(d)
         pltpu.make_async_remote_copy(
-            returning.at[pl.ds((a * N_GY + b) * 2, 2)], arrived_back.at[pl.ds(me * 2, 2)],
+            returning.at[pl.ds(d * 2, 2)], arrived_back.at[pl.ds(me * 2, 2)],
             a2a_sem.at[2], a2a_sem.at[3], device_id=(a, b), device_id_type=MESH,
         ).start()
 
     each_peer(send_back)
+    pack_back(me)
     for h in range(2):
         arrived_back[me * 2 + h] = returning[me * 2 + h]
+    to_grid_order(2, 3)
 
     def finish(i, carry):
         rows = aligned(HALO + i * 8)
@@ -559,8 +588,11 @@
             pltpu.VMEM((8, N_DEV), i32),
             pltpu.SMEM((8, N_DEV), i32),
             pltpu.VMEM((N_DEV, 4, 8, 128), f32),
-            pltpu.VMEM((2 * N_DEV, 4, 8, 128), f32),
-            pltpu.VMEM((2 * N_DEV, 4, 8, 128), f32),
+            pltpu.VMEM((N_DEV, 8, 128), f32),
+            pltpu.VMEM((2 * N_DEV, 8, 128), f32),
+            pltpu.VMEM((2 * N_DEV, 8, 128), f32),
+            pltpu.VMEM((2 * N_DEV, 2, 8, 128), f32),
+            pltpu.VMEM((2 * N_DEV, 2, 8, 128), f32),
             pltpu.VMEM((FIELDS, CT, EXT, 128), f32),
             pltpu.VMEM((TILES_X, ROWS, 128), i32),
             side, side, side, side,
@@ -573,8 +605,8 @@
             pltpu.VMEM((2 * N_DEV, 2, 8, 128), f32),
             ghosted, ghosted, ghosted, ghosted, ghosted, ghosted,
             plain, plain, plain, plain, plain, plain,
-            pltpu.SemaphoreType.DMA((5,)),
-            pltpu.SemaphoreType.DMA((4,)),
+            pltpu.SemaphoreType.DMA((6,)),
+            pltpu.SemaphoreType.DMA((6,)),
             pltpu.SemaphoreType.DMA((20,)),
         ],
         compiler_params=pltpu.CompilerParams(

time: 164 us -> 159 us (0.970)
  Pallas kernels: 160 us -> 154 us
    pallas_call x1, Pallas kernels: 160 us -> 154 us  [local(): pl.pallas_call(kernel, out_shape=(jax.ShapeDtypeStruct((N_DEV, 2, 8, 128)...]
where the time goes in v4:
time: 159 us; the launch traced here: 158 us
  Pallas kernels  154 us (97%)
  local copies, waits for them, and re-layouts  3.53 us (2%)
    pallas_call x1, Pallas kernels, local(): pl.pallas_call(kernel, out_shape=(jax.ShapeDtypeStruct((N_DEV, 2, 8, 128)...  154 us
    unnamed x4, local copies, waits for them, and re-layouts  3.53 us

profile of v4, /device:TPU:1, one launch (start us, length us, event | category | flops | bytes accessed | tf_op | source)
XLA Modules:
  0.0 158.2 jit_solution(15998587255688260641)
XLA Ops:
  0.6 154.0 %shard_map.86 = (f32[128,2,8,128]{3,2,1,0:T(8,128)}, f32[3,128,1024]{2,1,0:T(8,128)}) custom-call(s32[128,128]{1,0:T(8,128)} %bitcast.1, f32[128,4,8,128]{3,2,1,0:T(8,128)} %ocean.1, s32[128,1024]{1,0:T(8,128)} %mask.1, f32[128,1024]{1,0:T(8,128)} %mass.1, f32[128,1024]{1,0:T(8,128)} %strength.1, f32[2,128,1024]{2,1,0:T(8,128)} %velocity.1, ...), custom_call_target="tpu_custom_call" | custom-call | tf_op jit(solution)/shard_map/pallas_call | solution.py:578
  154.6 0.0 copy-start
  154.6 2.4 %copy.11 = f32[128,2,8,128]{3,2,1,0:T(8,128)} copy(f32[128,2,8,128]{3,2,1,0:T(8,128)} %get-tuple-element.4) | data formatting | bytes 2097152
  157.0 0.0 copy-done
  157.0 1.1 copy.12
Async XLA Ops:
  154.6 2.4 %copy-start = (f32[3,128,1024]{2,1,0:T(8,128)S(1)}, f32[3,128,1024]{2,1,0:T(8,128)}, u32[]{:S(2)}) copy-start(f32[3,128,1024]{2,1,0:T(8,128)} %get-tuple-element.5) | copy-start | bytes 4718596

commit v5 on v4

--- a/solution.py
+++ b/solution.py
@@ -44,7 +44,7 @@
     return order
 
 
-def each_peer(visit, first=0, last=4):
+def each_peer(visit, between=()):
     gx = lax.axis_index("gx")
     gy = lax.axis_index("gy")
     z, x_lo = gx % 4, gx // 4
@@ -55,10 +55,13 @@
     part_gy = [(v // 2) * 8 for v in xs]
     ys = [((y + d) % 4) * 2 for d in range(4)]
     cores = [core, 1 - core]
-    zs = tuple((z + d + first) % 4 for d in range(4))
+    zs = tuple((z + d) % 4 for d in range(4))
 
     def turn(q, zs):
-        for dx, dy, dc, off in peers():
+        for n, (dx, dy, dc, off) in enumerate(peers()):
+            for i, extra in enumerate(between):
+                if n == (2 * i + 1) * 16 // len(between):
+                    extra(q)
             there = (part_gx[dx] + zs[off], part_gy[dx] + ys[dy] + cores[dc])
             if (dx, dy, dc) == (0, 0, 0):
                 pl.when(q > 0)(functools.partial(visit, *there))
@@ -66,7 +69,7 @@
                 visit(*there)
         return zs[1:] + zs[:1]
 
-    lax.fori_loop(first, last, turn, zs)
+    lax.fori_loop(0, 4, turn, zs)
 
 
 def wait_for(ref, sem):
@@ -229,19 +232,25 @@
     north_gy = jnp.minimum(gy + 1, N_GY - 1)
     south_gy = jnp.maximum(gy - 1, 0)
 
-    def rows_start(upper, lower, south, north, sems):
+    def rows_north(upper, lower, south, north, sems):
         to_north = pltpu.make_async_remote_copy(
             upper, south, halo_sem.at[sems], halo_sem.at[sems + 1],
             device_id=(gx, north_gy), device_id_type=MESH)
         to_partner = pltpu.make_async_remote_copy(
             upper, north, halo_sem.at[sems], halo_sem.at[sems + 3],
             device_id=(N_GX - 1 - gx, gy), device_id_type=MESH)
+        pl.when(jnp.logical_not(top))(to_north.start)
+        pl.when(top)(to_partner.start)
+
+    def rows_south(upper, lower, south, north, sems):
         to_south = pltpu.make_async_remote_copy(
             lower, north, halo_sem.at[sems + 2], halo_sem.at[sems + 3],
             device_id=(gx, south_gy), device_id_type=MESH)
-        pl.when(jnp.logical_not(top))(to_north.start)
-        pl.when(top)(to_partner.start)
         pl.when(gy > 0)(to_south.start)
+
+    def rows_start(*args):
+        rows_north(*args)
+        rows_south(*args)
 
     def rows_wait(upper, lower, south, north, sems):
         wait_for(north, halo_sem.at[sems + 3])
@@ -252,9 +261,10 @@
             wait_for(south, halo_sem.at[sems + 1])
             wait_for(lower, halo_sem.at[sems + 2])
 
-    def strips(first, count):
+    def strips(first, count, tile=0, tiles=CT):
         return tuple(
-            ext.at[pl.ds(first, count), :, pl.ds(at, HALO)] for at in (ROWS, HALO, 0, HALO + ROWS))
+            ext.at[pl.ds(first, count), pl.ds(tile, tiles), pl.ds(at, HALO)]
+            for at in (ROWS, HALO, 0, HALO + ROWS))
 
     back_sub = 7 - lax.broadcasted_iota(jnp.int32, (8, 128), 0)
     back_lane = 127 - lane
@@ -310,17 +320,23 @@
 
     for copy in static_cols:
         copy.start()
-    each_peer(send_mass)
+    each_peer(send_mass, (
+        lambda q: rows_north(*strips(q, 1, 0, TILES_X), 8),
+        lambda q: rows_south(*strips(q, 1, 0, TILES_X), 8),
+    ))
     for h in range(2):
         mass_in[me * 2 + h] = mass_out[me * 2 + h]
     for copy in static_cols:
         copy.wait()
     spread_columns(0, STATIC, from_west, from_east)
-    rows_start(*static_rows, 8)
 
     wait_for(oc, in_sem.at[0])
     wait_for(mass_in.at[pl.ds(0, 2 * N_DEV - 2)], a2a_sem.at[5])
-    each_peer(send_forces)
+    rows_start(*strips(0, STATIC, TILES_X, 1), 8)
+    each_peer(send_forces, (
+        lambda q: rows_north(*strips(4 + q, 1, 0, TILES_X), 8),
+        lambda q: rows_south(*strips(4 + q, 1, 0, TILES_X), 8),
+    ))
     pack_forces(me)
     for h in range(2):
         arrived[me * 2 + h] = outgoing[me * 2 + h]
@@ -392,10 +408,11 @@
     gather_columns(FORCE_X, 2, force_to_east, force_to_west)
     for copy in force_cols:
         copy.start()
+    rows_start(*strips(FORCE_X, 2, 0, TILES_X), 12)
     for copy in force_cols:
         copy.wait()
     spread_columns(FORCE_X, 2, force_from_west, force_from_east)
-    rows_start(*force_rows, 12)
+    rows_start(*strips(FORCE_X, 2, TILES_X, 1), 12)
     rows_wait(*force_rows, 12)
 
     @pl.when(top)
@@ -486,8 +503,11 @@
         lax.fori_loop(0, CT, body, 0)
 
     def exchange_rows():
-        to_grid_order(0, 5)
-        rows_start(*state_rows, 16)
+        for f in range(5):
+            to_grid_order(f, 1)
+            rows_start(
+                nat.at[f, :, pl.ds(ROWS, HALO)], nat.at[f, :, pl.ds(HALO, HALO)],
+                from_south.at[f], from_north.at[f], 16)
         rows_wait(*state_rows, 16)
 
         @pl.when(top)

time: 159 us -> 144 us (0.906)
  Pallas kernels: 154 us -> 140 us
    pallas_call x1, Pallas kernels: 154 us -> 140 us  [local(): pl.pallas_call(kernel, out_shape=(jax.ShapeDtypeStruct((N_DEV, 2, 8, 128)...]
where the time goes in v5:
time: 144 us
  Pallas kernels  140 us (97%)
  local copies, waits for them, and re-layouts  3.53 us (2%)
    pallas_call x1, Pallas kernels, local(): pl.pallas_call(kernel, out_shape=(jax.ShapeDtypeStruct((N_DEV, 2, 8, 128)...  140 us
    unnamed x4, local copies, waits for them, and re-layouts  3.53 us

profile of v5, /device:TPU:1, one launch (start us, length us, event | category | flops | bytes accessed | tf_op | source)
XLA Modules:
  0.0 144.2 jit_solution(12229135854665287348)
XLA Ops:
  0.6 140.0 %shard_map.86 = (f32[128,2,8,128]{3,2,1,0:T(8,128)}, f32[3,128,1024]{2,1,0:T(8,128)}) custom-call(s32[128,128]{1,0:T(8,128)} %bitcast.1, f32[128,4,8,128]{3,2,1,0:T(8,128)} %ocean.1, s32[128,1024]{1,0:T(8,128)} %mask.1, f32[128,1024]{1,0:T(8,128)} %mass.1, f32[128,1024]{1,0:T(8,128)} %strength.1, f32[2,128,1024]{2,1,0:T(8,128)} %velocity.1, ...), custom_call_target="tpu_custom_call" | custom-call | tf_op jit(solution)/shard_map/pallas_call | solution.py:598
  140.7 0.0 copy-start
  140.7 2.4 %copy.11 = f32[128,2,8,128]{3,2,1,0:T(8,128)} copy(f32[128,2,8,128]{3,2,1,0:T(8,128)} %get-tuple-element.4) | data formatting | bytes 2097152
  143.1 0.0 copy-done
  143.1 1.1 copy.12
Async XLA Ops:
  140.7 2.4 %copy-start = (f32[3,128,1024]{2,1,0:T(8,128)S(1)}, f32[3,128,1024]{2,1,0:T(8,128)}, u32[]{:S(2)}) copy-start(f32[3,128,1024]{2,1,0:T(8,128)} %get-tuple-element.5) | copy-start | bytes 4718596

commit v6 on v5

--- a/solution.py
+++ b/solution.py
@@ -26,7 +26,7 @@
 STEP = EXT // 8
 TILES_X = 8
 CT = TILES_X + 1
-UNROLL = 10
+UNROLL = 20
 
 MASS, STRENGTH, ZONAL, MERID, SUM, DIFF, SHEAR, SHARE, FORCE_X, FORCE_Y = range(10)
 STATIC = 8
@@ -177,14 +177,6 @@
 
     lax.fori_loop(0, N_DEV // 8, pack_mass, 0)
 
-    wait_for(ext_mask, in_sem.at[2])
-
-    def shares(i, carry):
-        for j in range(TILES_X):
-            ext[SHARE, j, aligned(HALO + i * 8)] = ext_mask[j, aligned(i * 8)].astype(jnp.float32)
-        return carry
-
-    lax.fori_loop(0, ROWS // 8, shares, 0)
     wait_for(ext.at[pl.ds(STRENGTH, STATIC - 2), pl.ds(0, TILES_X), inner], in_sem.at[1])
 
     def gather_columns(first, count, east_out, west_out):
@@ -293,8 +285,6 @@
     static_rows = strips(0, STATIC)
     force_rows = strips(FORCE_X, 2)
 
-    gather_columns(0, STATIC, to_east, to_west)
-
     pl.semaphore_wait(barrier, N_DEV - 1)
 
     def send_mass(a, b):
@@ -318,14 +308,23 @@
             a2a_sem.at[0], a2a_sem.at[1], device_id=(a, b), device_id_type=MESH,
         ).start()
 
-    for copy in static_cols:
-        copy.start()
     each_peer(send_mass, (
         lambda q: rows_north(*strips(q, 1, 0, TILES_X), 8),
         lambda q: rows_south(*strips(q, 1, 0, TILES_X), 8),
     ))
     for h in range(2):
         mass_in[me * 2 + h] = mass_out[me * 2 + h]
+    wait_for(ext_mask, in_sem.at[2])
+
+    def shares(i, carry):
+        for j in range(TILES_X):
+            ext[SHARE, j, aligned(HALO + i * 8)] = ext_mask[j, aligned(i * 8)].astype(jnp.float32)
+        return carry
+
+    lax.fori_loop(0, ROWS // 8, shares, 0)
+    gather_columns(0, STATIC, to_east, to_west)
+    for copy in static_cols:
+        copy.start()
     for copy in static_cols:
         copy.wait()
     spread_columns(0, STATIC, from_west, from_east)

time: 144 us -> 137 us (0.951)
  Pallas kernels: 140 us -> 133 us
    pallas_call x1, Pallas kernels: 140 us -> 133 us  [local(): pl.pallas_call(kernel, out_shape=(jax.ShapeDtypeStruct((N_DEV, 2, 8, 128)...]
where the time goes in v6:
time: 137 us
  Pallas kernels  133 us (97%)
  local copies, waits for them, and re-layouts  3.53 us (3%)
    pallas_call x1, Pallas kernels, local(): pl.pallas_call(kernel, out_shape=(jax.ShapeDtypeStruct((N_DEV, 2, 8, 128)...  133 us
    unnamed x4, local copies, waits for them, and re-layouts  3.53 us

profile of v6, /device:TPU:1, one launch (start us, length us, event | category | flops | bytes accessed | tf_op | source)
XLA Modules:
  0.0 136.9 jit_solution(7984509331020007284)
XLA Ops:
  0.6 132.7 %shard_map.86 = (f32[128,2,8,128]{3,2,1,0:T(8,128)}, f32[3,128,1024]{2,1,0:T(8,128)}) custom-call(s32[128,128]{1,0:T(8,128)} %bitcast.1, f32[128,4,8,128]{3,2,1,0:T(8,128)} %ocean.1, s32[128,1024]{1,0:T(8,128)} %mask.1, f32[128,1024]{1,0:T(8,128)} %mass.1, f32[128,1024]{1,0:T(8,128)} %strength.1, f32[2,128,1024]{2,1,0:T(8,128)} %velocity.1, ...), custom_call_target="tpu_custom_call" | custom-call | tf_op jit(solution)/shard_map/pallas_call | solution.py:597
  133.3 0.0 copy-start
  133.4 2.4 %copy.11 = f32[128,2,8,128]{3,2,1,0:T(8,128)} copy(f32[128,2,8,128]{3,2,1,0:T(8,128)} %get-tuple-element.4) | data formatting | bytes 2097152
  135.7 0.0 copy-done
  135.7 1.1 copy.12
Async XLA Ops:
  133.3 2.4 %copy-start = (f32[3,128,1024]{2,1,0:T(8,128)S(1)}, f32[3,128,1024]{2,1,0:T(8,128)}, u32[]{:S(2)}) copy-start(f32[3,128,1024]{2,1,0:T(8,128)} %get-tuple-element.5) | copy-start | bytes 4718596

commit v7 on v5

--- a/solution.py
+++ b/solution.py
@@ -26,7 +26,7 @@
 STEP = EXT // 8
 TILES_X = 8
 CT = TILES_X + 1
-UNROLL = 10
+UNROLL = 20
 
 MASS, STRENGTH, ZONAL, MERID, SUM, DIFF, SHEAR, SHARE, FORCE_X, FORCE_Y = range(10)
 STATIC = 8
@@ -185,6 +185,7 @@
         return carry
 
     lax.fori_loop(0, ROWS // 8, shares, 0)
+
     wait_for(ext.at[pl.ds(STRENGTH, STATIC - 2), pl.ds(0, TILES_X), inner], in_sem.at[1])
 
     def gather_columns(first, count, east_out, west_out):
@@ -293,8 +294,6 @@
     static_rows = strips(0, STATIC)
     force_rows = strips(FORCE_X, 2)
 
-    gather_columns(0, STATIC, to_east, to_west)
-
     pl.semaphore_wait(barrier, N_DEV - 1)
 
     def send_mass(a, b):
@@ -318,14 +317,17 @@
             a2a_sem.at[0], a2a_sem.at[1], device_id=(a, b), device_id_type=MESH,
         ).start()
 
-    for copy in static_cols:
-        copy.start()
     each_peer(send_mass, (
-        lambda q: rows_north(*strips(q, 1, 0, TILES_X), 8),
-        lambda q: rows_south(*strips(q, 1, 0, TILES_X), 8),
+        lambda q: rows_north(*strips(2 * q, 1, 0, TILES_X), 8),
+        lambda q: rows_south(*strips(2 * q, 1, 0, TILES_X), 8),
+        lambda q: rows_north(*strips(2 * q + 1, 1, 0, TILES_X), 8),
+        lambda q: rows_south(*strips(2 * q + 1, 1, 0, TILES_X), 8),
     ))
     for h in range(2):
         mass_in[me * 2 + h] = mass_out[me * 2 + h]
+    gather_columns(0, STATIC, to_east, to_west)
+    for copy in static_cols:
+        copy.start()
     for copy in static_cols:
         copy.wait()
     spread_columns(0, STATIC, from_west, from_east)
@@ -333,10 +335,7 @@
     wait_for(oc, in_sem.at[0])
     wait_for(mass_in.at[pl.ds(0, 2 * N_DEV - 2)], a2a_sem.at[5])
     rows_start(*strips(0, STATIC, TILES_X, 1), 8)
-    each_peer(send_forces, (
-        lambda q: rows_north(*strips(4 + q, 1, 0, TILES_X), 8),
-        lambda q: rows_south(*strips(4 + q, 1, 0, TILES_X), 8),
-    ))
+    each_peer(send_forces)
     pack_forces(me)
     for h in range(2):
         arrived[me * 2 + h] = outgoing[me * 2 + h]
@@ -393,6 +392,15 @@
 
     ghosts(cu, cv, cstr)
 
+    def gradient(r, carry):
+        left, right = left_right([cstr[r + 1, j] for j in range(CT)], lane)
+        for j in range(CT):
+            kfx[r, j] = -0.25 * (right[j] - left[j])
+            kfy[r, j] = -0.25 * (cstr[r + 2, j] - cstr[r, j])
+        return carry
+
+    lax.fori_loop(0, STEP, gradient, 0)
+
     wait_for(arrived.at[pl.ds(0, 2 * N_DEV - 2)], a2a_sem.at[1])
     wait_for(outgoing.at[pl.ds(0, 2 * N_DEV - 2)], a2a_sem.at[0])
 
@@ -409,25 +417,25 @@
     for copy in force_cols:
         copy.start()
     rows_start(*strips(FORCE_X, 2, 0, TILES_X), 12)
-    for copy in force_cols:
-        copy.wait()
-    spread_columns(FORCE_X, 2, force_from_west, force_from_east)
-    rows_start(*strips(FORCE_X, 2, TILES_X, 1), 12)
-    rows_wait(*force_rows, 12)
-
-    @pl.when(top)
-    def _():
-        fold(ext, FORCE_X, 2, HALO + ROWS, (FORCE_X, FORCE_Y + 1))
-
     def arrange_forces(r, carry):
         rows = pl.ds(r, 8, stride=STEP)
-        left, right = left_right([cstr[r + 1, j] for j in range(CT)], lane)
         for j in range(CT):
-            kfx[r, j] = ext[FORCE_X, j, rows] - 0.25 * (right[j] - left[j])
-            kfy[r, j] = ext[FORCE_Y, j, rows] - 0.25 * (cstr[r + 2, j] - cstr[r, j])
-        return carry
-
-    lax.fori_loop(0, STEP, arrange_forces, 0)
+            kfx[r, j] += ext[FORCE_X, j, rows]
+            kfy[r, j] += ext[FORCE_Y, j, rows]
+        return carry
+
+    def take_forces():
+        for copy in force_cols:
+            copy.wait()
+        spread_columns(FORCE_X, 2, force_from_west, force_from_east)
+        rows_start(*strips(FORCE_X, 2, TILES_X, 1), 12)
+        rows_wait(*force_rows, 12)
+
+        @pl.when(top)
+        def _():
+            fold(ext, FORCE_X, 2, HALO + ROWS, (FORCE_X, FORCE_Y + 1))
+
+        lax.fori_loop(0, STEP, arrange_forces, 0)
 
     def shifted(ref, r):
         def left(j):
@@ -502,12 +510,15 @@
 
         lax.fori_loop(0, CT, body, 0)
 
-    def exchange_rows():
-        for f in range(5):
+    def send_rows(first, count):
+        for f in range(first, first + count):
             to_grid_order(f, 1)
             rows_start(
                 nat.at[f, :, pl.ds(ROWS, HALO)], nat.at[f, :, pl.ds(HALO, HALO)],
                 from_south.at[f], from_north.at[f], 16)
+
+    def exchange_rows():
+        send_rows(0, 2)
         rows_wait(*state_rows, 16)
 
         @pl.when(top)
@@ -524,11 +535,13 @@
         ghosts(cu, cv)
 
     def subcycle(t, carry):
-        pl.when(t == ITERS // LEGS)(exchange_rows)
         lax.fori_loop(0, STEP // UNROLL, stresses, 0)
+        pl.when(t == 0)(take_forces)
+        pl.when(t == ITERS // LEGS - 1)(lambda: send_rows(2, 3))
         ghosts(cyy, csh)
         lax.fori_loop(0, STEP // UNROLL, momentum, 0)
         ghosts(cu, cv)
+        pl.when(t == ITERS // LEGS - 1)(exchange_rows)
         return carry
 
     lax.fori_loop(0, ITERS, subcycle, 0)

time: 144 us -> 134 us (0.931)
  Pallas kernels: 140 us -> 129 us
    pallas_call x1, Pallas kernels: 140 us -> 129 us  [local(): pl.pallas_call(kernel, out_shape=(jax.ShapeDtypeStruct((N_DEV, 2, 8, 128)...]
where the time goes in v7:
time: 134 us
  Pallas kernels  129 us (96%)
  local copies, waits for them, and re-layouts  3.53 us (3%)
    pallas_call x1, Pallas kernels, local(): pl.pallas_call(kernel, out_shape=(jax.ShapeDtypeStruct((N_DEV, 2, 8, 128)...  129 us
    unnamed x4, local copies, waits for them, and re-layouts  3.53 us

profile of v7, /device:TPU:1, one launch (start us, length us, event | category | flops | bytes accessed | tf_op | source)
XLA Modules:
  0.0 133.5 jit_solution(1812504442840554075)
XLA Ops:
  0.6 129.3 %shard_map.86 = (f32[128,2,8,128]{3,2,1,0:T(8,128)}, f32[3,128,1024]{2,1,0:T(8,128)}) custom-call(s32[128,128]{1,0:T(8,128)} %bitcast.1, f32[128,4,8,128]{3,2,1,0:T(8,128)} %ocean.1, s32[128,1024]{1,0:T(8,128)} %mask.1, f32[128,1024]{1,0:T(8,128)} %mass.1, f32[128,1024]{1,0:T(8,128)} %strength.1, f32[2,128,1024]{2,1,0:T(8,128)} %velocity.1, ...), custom_call_target="tpu_custom_call" | custom-call | tf_op jit(solution)/shard_map/pallas_call | solution.py:611
  130.0 0.0 copy-start
  130.0 2.4 %copy.11 = f32[128,2,8,128]{3,2,1,0:T(8,128)} copy(f32[128,2,8,128]{3,2,1,0:T(8,128)} %get-tuple-element.4) | data formatting | bytes 2097152
  132.4 0.0 copy-done
  132.4 1.1 copy.12
Async XLA Ops:
  130.0 2.4 %copy-start = (f32[3,128,1024]{2,1,0:T(8,128)S(1)}, f32[3,128,1024]{2,1,0:T(8,128)}, u32[]{:S(2)}) copy-start(f32[3,128,1024]{2,1,0:T(8,128)} %get-tuple-element.5) | copy-start | bytes 4718596

commit v8 on v7

--- a/solution.py
+++ b/solution.py
@@ -74,6 +74,15 @@
 
 def wait_for(ref, sem):
     pltpu.make_async_copy(ref, ref, sem).wait()
+
+
+def steps(count, body, by):
+    def several(i, carry):
+        for h in range(by):
+            body(i * by + h, carry)
+        return carry
+
+    lax.fori_loop(0, count // by, several, 0)
 
 
 def aligned(start, size=8):
@@ -166,7 +175,7 @@
             mass_tiles[i * TILES_X + j] = ext[MASS, j, aligned(HALO + i * 8)]
         return carry
 
-    lax.fori_loop(0, ROWS // 8, to_mass_tiles, 0)
+    steps(ROWS // 8, to_mass_tiles, 4)
     to_place.wait()
 
     def pack_mass(i, carry):
@@ -175,7 +184,7 @@
             mass_out[i * 16 + 2 * h + 1] = mass_tiles[place[LATE, i * 8 + h]]
         return carry
 
-    lax.fori_loop(0, N_DEV // 8, pack_mass, 0)
+    steps(N_DEV // 8, pack_mass, 2)
 
     wait_for(ext_mask, in_sem.at[2])
 
@@ -184,7 +193,7 @@
             ext[SHARE, j, aligned(HALO + i * 8)] = ext_mask[j, aligned(i * 8)].astype(jnp.float32)
         return carry
 
-    lax.fori_loop(0, ROWS // 8, shares, 0)
+    steps(ROWS // 8, shares, 4)
 
     wait_for(ext.at[pl.ds(STRENGTH, STATIC - 2), pl.ds(0, TILES_X), inner], in_sem.at[1])
 
@@ -205,7 +214,7 @@
                 west_out[g, aligned(i * 8)] = w
             return carry
 
-        lax.fori_loop(0, ROWS // 8, body, 0)
+        steps(ROWS // 8, body, 4)
 
     def spread_columns(first, count, west_in, east_in):
         def body(i, carry):
@@ -219,7 +228,7 @@
                     ext[first + 4 * g + q, TILES_X, rows] = jnp.where(lane < 64, right, left)
             return carry
 
-        lax.fori_loop(0, ROWS // 8, body, 0)
+        steps(ROWS // 8, body, 4)
 
     def columns(east_out, west_out, west_in, east_in, sems):
         a = pltpu.make_async_remote_copy(
@@ -382,7 +391,7 @@
             csh[r + 1, j] = 0.5 * ext[SHEAR, j, rows]
         return carry
 
-    lax.fori_loop(0, STEP, arrange, 0)
+    steps(STEP, arrange, 2)
 
     def ghosts(*refs):
         for ref in refs:
@@ -399,7 +408,7 @@
             kfy[r, j] = -0.25 * (cstr[r + 2, j] - cstr[r, j])
         return carry
 
-    lax.fori_loop(0, STEP, gradient, 0)
+    steps(STEP, gradient, 2)
 
     wait_for(arrived.at[pl.ds(0, 2 * N_DEV - 2)], a2a_sem.at[1])
     wait_for(outgoing.at[pl.ds(0, 2 * N_DEV - 2)], a2a_sem.at[0])
@@ -412,7 +421,7 @@
             ext[FORCE_Y, j, rows] = tile[1]
         return carry
 
-    lax.fori_loop(0, ROWS // 8, forces, 0)
+    steps(ROWS // 8, forces, 4)
     gather_columns(FORCE_X, 2, force_to_east, force_to_west)
     for copy in force_cols:
         copy.start()
@@ -435,7 +444,7 @@
         def _():
             fold(ext, FORCE_X, 2, HALO + ROWS, (FORCE_X, FORCE_Y + 1))
 
-        lax.fori_loop(0, STEP, arrange_forces, 0)
+        steps(STEP, arrange_forces, 5)
 
     def shifted(ref, r):
         def left(j):
@@ -491,7 +500,7 @@
                     nat[f, j, pl.ds(r, 8, stride=STEP)] = carried[f][r + 1, j]
             return carry
 
-        lax.fori_loop(0, STEP, body, 0)
+        steps(STEP, body, 5)
 
     def from_grid_order(r, carry):
         for f, ref in enumerate(carried):
@@ -508,7 +517,7 @@
                     nat[f, j, pl.ds(base + p * 8, 8)] = strip[f, j, pl.ds(p * 8, 8)]
             return carry
 
-        lax.fori_loop(0, CT, body, 0)
+        steps(CT, body, 3)
 
     def send_rows(first, count):
         for f in range(first, first + count):
@@ -531,7 +540,7 @@
         def _():
             take(from_south, 0)
 
-        lax.fori_loop(0, STEP, from_grid_order, 0)
+        steps(STEP, from_grid_order, 4)
         ghosts(cu, cv)
 
     def subcycle(t, carry):
@@ -554,7 +563,7 @@
             tiles[i * TILES_X + j, 1] = nat[1, j, rows]
         return carry
 
-    lax.fori_loop(0, ROWS // 8, to_tiles, 0)
+    steps(ROWS // 8, to_tiles, 4)
 
     def pack_back(d):
         returning[d * 2] = tiles[place[EARLY, d]]
@@ -584,7 +593,7 @@
             final[2, j, aligned(i * 8)] = 2.0 * nat[4, j, rows]
         return carry
 
-    lax.fori_loop(0, ROWS // 8, finish, 0)
+    steps(ROWS // 8, finish, 2)
     for j in range(TILES_X):
         pltpu.make_async_copy(final.at[:, j], out_stress.at[:, :, pl.ds(j * 128, 128)], in_sem.at[1]).start()
 
@@ -596,7 +605,7 @@
             out_velocity[i * 8 + h] = arrived_back[place[BACK_SLOT, i * 8 + h]]
         return carry
 
-    lax.fori_loop(0, N_DEV // 8, unpack, 0)
+    steps(N_DEV // 8, unpack, 4)
     wait_for(final, in_sem.at[1])
 
 

time: 134 us -> 131 us (0.978)
  Pallas kernels: 129 us -> 127 us
    pallas_call x1, Pallas kernels: 129 us -> 127 us  [local(): pl.pallas_call(kernel, out_shape=(jax.ShapeDtypeStruct((N_DEV, 2, 8, 128)...]
where the time goes in v8:
time: 131 us
  Pallas kernels  127 us (97%)
  local copies, waits for them, and re-layouts  3.53 us (3%)
    pallas_call x1, Pallas kernels, local(): pl.pallas_call(kernel, out_shape=(jax.ShapeDtypeStruct((N_DEV, 2, 8, 128)...  127 us
    unnamed x4, local copies, waits for them, and re-layouts  3.53 us

profile of v8, /device:TPU:1, one launch (start us, length us, event | category | flops | bytes accessed | tf_op | source)
XLA Modules:
  0.0 131.0 jit_solution(3203916474809096304)
XLA Ops:
  0.6 126.8 %shard_map.86 = (f32[128,2,8,128]{3,2,1,0:T(8,128)}, f32[3,128,1024]{2,1,0:T(8,128)}) custom-call(s32[128,128]{1,0:T(8,128)} %bitcast.1, f32[128,4,8,128]{3,2,1,0:T(8,128)} %ocean.1, s32[128,1024]{1,0:T(8,128)} %mask.1, f32[128,1024]{1,0:T(8,128)} %mass.1, f32[128,1024]{1,0:T(8,128)} %strength.1, f32[2,128,1024]{2,1,0:T(8,128)} %velocity.1, ...), custom_call_target="tpu_custom_call" | custom-call | tf_op jit(solution)/shard_map/pallas_call | solution.py:620
  127.5 0.0 copy-start
  127.5 2.4 %copy.11 = f32[128,2,8,128]{3,2,1,0:T(8,128)} copy(f32[128,2,8,128]{3,2,1,0:T(8,128)} %get-tuple-element.4) | data formatting | bytes 2097152
  129.9 0.0 copy-done
  129.9 1.1 copy.12
Async XLA Ops:
  127.5 2.4 %copy-start = (f32[3,128,1024]{2,1,0:T(8,128)S(1)}, f32[3,128,1024]{2,1,0:T(8,128)}, u32[]{:S(2)}) copy-start(f32[3,128,1024]{2,1,0:T(8,128)} %get-tuple-element.5) | copy-start | bytes 4718596
